TPU v7x, 32 devices: a whole 2x2x4 slice. The times are simulated.
32 devices in a mesh: chan: 4 (over x, core), frames: 8 (over z, y).
Axes of the slice: x: 2, y: 2, z: 4, core: 2. Of those that a mesh axis runs over, the one named last changes fastest.
Arguments:
- signal: bfloat16 [2688, 8192], P('frames', 'chan'), may hold values from -7.2 to 7.2
- clip_ids: int32 [2688], P('frames'), may hold values from 0 to 4, never falling along the last dimension, each value on 1 to 1075 neighbouring positions
- output_grad: bfloat16 [2688, 8192], P('frames', 'chan'), may hold values from -8.4 to 8.4
- first_weight: float32 [1280, 256], P('frames', 'chan'), may hold values from -0.1875 to 0.1875
- first_mean: float32 [1280, 256], P('frames', 'chan'), may hold values from -0.046875 to 0.046875
- first_square: float32 [1280, 256], P('frames', 'chan'), may hold values from 4.7643007e-06 to 1.9057203e-05
- wide_weight: float32 [3, 2304, 256], P(None, 'frames', 'chan'), may hold values from -0.125 to 0.125
- wide_mean: float32 [3, 2304, 256], P(None, 'frames', 'chan'), may hold values from -0.046875 to 0.046875
- wide_square: float32 [3, 2304, 256], P(None, 'frames', 'chan'), may hold values from 4.7643007e-06 to 1.9057203e-05
- norm_params: float32 [2, 7, 128], P(None, None, 'chan'), may hold values from -1.2 to 2.6
- norm_mean: float32 [2, 7, 128], P(None, None, 'chan'), may hold values from -0.046875 to 0.046875
- norm_square: float32 [2, 7, 128], P(None, None, 'chan'), may hold values from 4.7643007e-06 to 1.9057203e-05
Outputs:
- block_out: float32 [2688, 8192], P('frames', 'chan')
- input_grad: float32 [2688, 8192], P('frames', 'chan')
- grad_norm: float32 [], replicated
- first_next: float32 [1280, 256], P('frames', 'chan')
- first_mean_next: float32 [1280, 256], P('frames', 'chan')
- first_square_next: float32 [1280, 256], P('frames', 'chan')
- first_rounded: bfloat16 [1280, 256], P('frames', 'chan')
- wide_next: float32 [3, 2304, 256], P(None, 'frames', 'chan')
- wide_mean_next: float32 [3, 2304, 256], P(None, 'frames', 'chan')
- wide_square_next: float32 [3, 2304, 256], P(None, 'frames', 'chan')
- wide_rounded: bfloat16 [3, 2304, 256], P(None, 'frames', 'chan')
- norm_next: float32 [2, 7, 128], P(None, None, 'chan')
- norm_mean_next: float32 [2, 7, 128], P(None, None, 'chan')
- norm_square_next: float32 [2, 7, 128], P(None, None, 'chan')
Inputs may be any that keep to these rules, and one draw needn't show every extreme that they name: `clip_ids`: clip number of each frame: 0 at the first frame, never falling, rising by one where a clip begins; every clip has 1 to 1075 frames.
All inputs are finite; a program needn't handle non-finite values.
Results may differ from a plain program's by a relative error of at most 0.024.
Values may be sent and summed in bfloat16 or wider, within the bound.
No kernel may reach another device: no remote copies, remote signals or barrier semaphores. Data moves between devices by JAX's collectives and lax.ppermute only.
A program may use at most 384 MiB of HBM per device.

v0:
```python
import jax
import jax.numpy as jnp
from jax import lax
from jax.sharding import PartitionSpec as P

B0 = 64
STEP = 10
B1 = 32


norm_epsilon = 1e-05
clip_limit = 100.0
beta_first = 0.9
beta_second = 0.999
adam_epsilon = 1e-08
conv_rate = 0.05
norm_rate = 0.5
weight_decay = 0.01


def padded_2(block, sides, width):
    for axis, dim in sides:
        count = lax.axis_size(axis)
        forward = [(i, i + 1) for i in range(count - 1)]
        backward = [(target, source) for source, target in forward]
        low = lax.ppermute(
            lax.slice_in_dim(block, block.shape[dim] - width, None, axis=dim), axis, forward
        )
        high = lax.ppermute(lax.slice_in_dim(block, 0, width, axis=dim), axis, backward)
        block = jnp.concatenate([low, block, high], axis=dim)
    return block


def edge_halo(values):
    return padded_2(values, (("frames", 0),), 1)


def spread_input(shard):
    padded = edge_halo(shard)
    return lax.all_gather(padded, "chan", axis=2, tiled=True)


def spread_grad(shard):
    padded = edge_halo(shard)
    return (padded, padded)


def to_channels(local_part, summed_over):
    if summed_over:
        return lax.psum_scatter(
            local_part.astype(jnp.bfloat16), "chan", scatter_dimension=2, tiled=True
        ).astype(jnp.float32)
    else:
        return local_part


def conv_local(padded, taps, masks, stride):
    frames = padded.shape[0] - 2
    out_bins = padded.shape[1] // stride
    widened = jnp.pad(padded, ((0, 0), (1, 1), (0, 0)))
    summed = None
    for time_tap in range(3):
        partial_sum = None
        for freq_tap in range(3):
            window = widened[
                time_tap : time_tap + frames,
                freq_tap : freq_tap + stride * (out_bins - 1) + 1 : stride,
            ]
            product = jnp.einsum(
                "fbi,io->fbo",
                window,
                taps[:, 3 * time_tap + freq_tap],
                preferred_element_type=jnp.float32,
            )
            partial_sum = product if partial_sum is None else partial_sum + product
        if time_tap == 0:
            partial_sum = partial_sum * masks[0]
        if time_tap == 2:
            partial_sum = partial_sum * masks[1]
        summed = partial_sum if summed is None else summed + partial_sum
    return summed


def shift_left(values):
    return jnp.concatenate([values[:, 1:], jnp.zeros_like(values[:, :1])], axis=1)


def shift_right(values):
    return jnp.concatenate([jnp.zeros_like(values[:, :1]), values[:, :-1]], axis=1)


def place_bins(pieces, stride):
    if stride == 1:
        return shift_left(pieces[0]) + pieces[1] + shift_right(pieces[2])
    odd_bins = pieces[2] + shift_left(pieces[0])
    frames, out_bins, channels = pieces[1].shape
    return jnp.stack([pieces[1], odd_bins], axis=2).reshape(frames, 2 * out_bins, channels)


def conv_grad_input(padded_grad, taps, masks, stride):
    frames = padded_grad.shape[0] - 2
    summed = None
    for time_tap in range(3):
        rows_used = padded_grad[2 - time_tap : 2 - time_tap + frames]
        pieces = [
            jnp.einsum(
                "fbo,io->fbi",
                rows_used,
                taps[:, 3 * time_tap + freq_tap],
                preferred_element_type=jnp.float32,
            )
            for freq_tap in range(3)
        ]
        placed = place_bins(pieces, stride)
        if time_tap == 0:
            placed = placed * masks[1]
        if time_tap == 2:
            placed = placed * masks[0]
        summed = placed if summed is None else summed + placed
    return summed


def conv_grad_weight(padded, grad_part, masks, stride):
    frames = grad_part.shape[0]
    out_bins = grad_part.shape[1]
    widened = jnp.pad(padded, ((0, 0), (1, 1), (0, 0)))
    weighted = [
        grad_part * masks[0].astype(jnp.bfloat16),
        grad_part,
        grad_part * masks[1].astype(jnp.bfloat16),
    ]
    columns = []
    for time_tap in range(3):
        for freq_tap in range(3):
            window = widened[
                time_tap : time_tap + frames,
                freq_tap : freq_tap + stride * (out_bins - 1) + 1 : stride,
            ]
            columns.append(
                jnp.einsum(
                    "fbi,fbo->io", window, weighted[time_tap], preferred_element_type=jnp.float32
                )
            )
    return jnp.stack(columns, axis=1)


def statistics(values):
    total_count = values.shape[0] * values.shape[1] * lax.axis_size("frames")
    moment_sums = lax.psum(
        (jnp.sum(values, axis=(0, 1)), jnp.sum(values * values, axis=(0, 1))), "frames"
    )
    average = moment_sums[0] / total_count
    inverse_spread = lax.rsqrt(moment_sums[1] / total_count - average * average + norm_epsilon)
    return (average, inverse_spread)


def activate(values, statistic, gain_bias):
    scaled = (values - statistic[0]) * statistic[1]
    return jax.nn.silu(scaled * gain_bias[0] + gain_bias[1])


def norm_backward(upstream, values, statistic, gain_bias):
    scaled = (values - statistic[0]) * statistic[1]
    pre_act = scaled * gain_bias[0] + gain_bias[1]
    sigmoid = jax.nn.sigmoid(pre_act)
    pre_grad = upstream * sigmoid * (1.0 + pre_act * (1.0 - sigmoid))
    total_count = values.shape[0] * values.shape[1] * lax.axis_size("frames")
    bias_grad, gain_grad = lax.psum(
        (jnp.sum(pre_grad, axis=(0, 1)), jnp.sum(pre_grad * scaled, axis=(0, 1))), "frames"
    )
    result = (
        gain_bias[0]
        * statistic[1]
        * (pre_grad - bias_grad / total_count - scaled * gain_grad / total_count)
    )
    return (result, gain_grad, bias_grad)


def norm_pair(params, norm_index):
    if norm_index == 0:
        return (params[0, 0], params[1, 0])
    row_pair = params[:, 2 * norm_index - 1 : 2 * norm_index + 1]
    packed = jnp.transpose(row_pair, (0, 2, 1)).reshape(2, -1)
    return (packed[0], packed[1])


def pack_norms(vectors):
    blocks = [vectors[0][None]]
    for vector in vectors[1:]:
        blocks.append(vector.reshape(-1, 2).T)
    return jnp.concatenate(blocks, axis=0)


def adam_step(weight, moment, square, gradient, step_rate, decay_rate):
    moment_next = beta_first * moment + (1.0 - beta_first) * gradient
    square_next = beta_second * square + (1.0 - beta_second) * gradient * gradient
    corrected = moment_next / (1.0 - beta_first**STEP)
    divisor = jnp.sqrt(square_next / (1.0 - beta_second**STEP)) + adam_epsilon
    weight_next = weight - step_rate * (corrected / divisor + decay_rate * weight)
    return (weight_next, moment_next, square_next)


def body(
    signal,
    clip_ids,
    output_grad,
    first_weight,
    first_mean,
    first_square,
    wide_weight,
    wide_mean,
    wide_square,
    norm_params,
    norm_mean,
    norm_square,
):
    frame_rows = signal.shape[0]
    padded_ids = padded_2(clip_ids + 1, (("frames", 0),), 1)
    centre_ids = padded_ids[1:-1]
    mask_prev = (padded_ids[:-2] == centre_ids).astype(jnp.float32)[:, None, None]
    mask_next = (padded_ids[2:] == centre_ids).astype(jnp.float32)[:, None, None]
    first_rows, wide_rows = (
        lax.all_gather(first_weight.astype(jnp.bfloat16), "frames", axis=0, tiled=True),
        lax.all_gather(wide_weight.astype(jnp.bfloat16), "frames", axis=1, tiled=True),
    )
    masks = (mask_prev, mask_next)
    in_channels = first_rows.shape[0] // 10
    wide_channels = wide_rows.shape[1] // 9
    out_columns = first_rows.shape[1]
    taps_first = first_rows[: 9 * in_channels].reshape(in_channels, 9, out_columns)
    short_taps = first_rows[9 * in_channels :]
    taps_wide = [
        wide_rows[layer_index].reshape(wide_channels, 9, out_columns) for layer_index in range(3)
    ]
    norm_pairs = [norm_pair(norm_params, norm_index) for norm_index in range(4)]
    signal_values = jnp.transpose(signal.astype(jnp.float32).reshape(frame_rows, -1, B0), (0, 2, 1))
    top_grad = jnp.transpose(output_grad.reshape(frame_rows, -1, B1), (0, 2, 1))
    stats_one = statistics(signal_values)
    spread_one = spread_input(
        activate(signal_values, stats_one, norm_pairs[0]).astype(jnp.bfloat16)
    )
    hidden_one = to_channels(conv_local(spread_one, taps_first, masks, 2), False)
    stats_two = statistics(hidden_one)
    spread_two = spread_input(activate(hidden_one, stats_two, norm_pairs[1]).astype(jnp.bfloat16))
    shortcut = jnp.einsum(
        "fbi,io->fbo", spread_one[1:-1, 0::2], short_taps, preferred_element_type=jnp.float32
    )
    residual = to_channels(conv_local(spread_two, taps_wide[0], masks, 1) + shortcut, False)
    stats_three = statistics(residual)
    spread_three = spread_input(activate(residual, stats_three, norm_pairs[2]).astype(jnp.bfloat16))
    hidden_two = to_channels(conv_local(spread_three, taps_wide[1], masks, 1), False)
    stats_four = statistics(hidden_two)
    spread_four = spread_input(activate(hidden_two, stats_four, norm_pairs[3]).astype(jnp.bfloat16))
    block_cube = residual + to_channels(conv_local(spread_four, taps_wide[2], masks, 1), False)
    top_weight_side, top_input_side = spread_grad(top_grad)
    weight_four = conv_grad_weight(spread_four, top_weight_side[1:-1], masks, 1)
    back_four = to_channels(conv_grad_input(top_input_side, taps_wide[2], masks, 1), True)
    grad_hidden_two, gain_four, bias_four = norm_backward(
        back_four, hidden_two, stats_four, norm_pairs[3]
    )
    hidden_two_weight_side, hidden_two_input_side = spread_grad(
        grad_hidden_two.astype(jnp.bfloat16)
    )
    weight_three = conv_grad_weight(spread_three, hidden_two_weight_side[1:-1], masks, 1)
    back_three = to_channels(conv_grad_input(hidden_two_input_side, taps_wide[1], masks, 1), True)
    grad_residual, gain_three, bias_three = norm_backward(
        back_three, residual, stats_three, norm_pairs[2]
    )
    residual_weight_side, residual_input_side = spread_grad(
        (top_grad.astype(jnp.float32) + grad_residual).astype(jnp.bfloat16)
    )
    weight_two = conv_grad_weight(spread_two, residual_weight_side[1:-1], masks, 1)
    short_grad = jnp.einsum(
        "fbi,fbo->io",
        spread_one[1:-1, 0::2],
        residual_weight_side[1:-1],
        preferred_element_type=jnp.float32,
    )
    back_two = to_channels(conv_grad_input(residual_input_side, taps_wide[0], masks, 1), True)
    grad_hidden_one, gain_two, bias_two = norm_backward(
        back_two, hidden_one, stats_two, norm_pairs[1]
    )
    hidden_one_weight_side, hidden_one_input_side = spread_grad(
        grad_hidden_one.astype(jnp.bfloat16)
    )
    weight_one = conv_grad_weight(spread_one, hidden_one_weight_side[1:-1], masks, 2)
    short_back = jnp.einsum(
        "fbo,io->fbi", residual_input_side[1:-1], short_taps, preferred_element_type=jnp.float32
    )
    short_placed = jnp.stack([short_back, jnp.zeros_like(short_back)], axis=2).reshape(
        short_back.shape[0], 2 * short_back.shape[1], short_back.shape[2]
    )
    back_one = to_channels(
        conv_grad_input(hidden_one_input_side, taps_first, masks, 2) + short_placed, True
    )
    input_cube, gain_one, bias_one = norm_backward(
        back_one, signal_values, stats_one, norm_pairs[0]
    )
    block_out = jnp.transpose(block_cube, (0, 2, 1)).reshape(frame_rows, -1)
    input_grad = jnp.transpose(input_cube, (0, 2, 1)).reshape(frame_rows, -1)
    grad_first = jnp.concatenate(
        [weight_one.reshape(9 * in_channels, out_columns), short_grad], axis=0
    )
    grad_wide = jnp.stack(
        [
            weight_two.reshape(9 * wide_channels, out_columns),
            weight_three.reshape(9 * wide_channels, out_columns),
            weight_four.reshape(9 * wide_channels, out_columns),
        ]
    )
    grad_first, grad_wide = (
        lax.psum_scatter(
            grad_first.astype(jnp.bfloat16), "frames", scatter_dimension=0, tiled=True
        ).astype(jnp.float32),
        lax.psum_scatter(
            grad_wide.astype(jnp.bfloat16), "frames", scatter_dimension=1, tiled=True
        ).astype(jnp.float32),
    )
    grad_norms = jnp.stack(
        [
            pack_norms([gain_one, gain_two, gain_three, gain_four]),
            pack_norms([bias_one, bias_two, bias_three, bias_four]),
        ]
    )
    own_squares = jnp.sum(grad_first * grad_first) + jnp.sum(grad_wide * grad_wide)
    own_squares = own_squares + jnp.where(
        lax.axis_index("frames") == 0, jnp.sum(grad_norms * grad_norms), 0.0
    )
    grad_norm = jnp.sqrt(lax.psum(own_squares, ("chan", "frames")))
    factor = clip_limit / jnp.maximum(grad_norm, clip_limit)
    first_next, first_mean_next, first_square_next = adam_step(
        first_weight, first_mean, first_square, grad_first * factor, conv_rate, weight_decay
    )
    wide_next, wide_mean_next, wide_square_next = adam_step(
        wide_weight, wide_mean, wide_square, grad_wide * factor, conv_rate, weight_decay
    )
    norm_next, norm_mean_next, norm_square_next = adam_step(
        norm_params, norm_mean, norm_square, grad_norms * factor, norm_rate, 0.0
    )
    return (
        block_out,
        input_grad,
        grad_norm,
        first_next,
        first_mean_next,
        first_square_next,
        first_next.astype(jnp.bfloat16),
        wide_next,
        wide_mean_next,
        wide_square_next,
        wide_next.astype(jnp.bfloat16),
        norm_next,
        norm_mean_next,
        norm_square_next,
    )


def solution(mesh):
    in_specs = (
        P("frames", "chan"),
        P("frames"),
        P("frames", "chan"),
        P("frames", "chan"),
        P("frames", "chan"),
        P("frames", "chan"),
        P(None, "frames", "chan"),
        P(None, "frames", "chan"),
        P(None, "frames", "chan"),
        P(None, None, "chan"),
        P(None, None, "chan"),
        P(None, None, "chan"),
    )
    out_specs = (
        P("frames", "chan"),
        P("frames", "chan"),
        P(),
        P("frames", "chan"),
        P("frames", "chan"),
        P("frames", "chan"),
        P("frames", "chan"),
        P(None, "frames", "chan"),
        P(None, "frames", "chan"),
        P(None, "frames", "chan"),
        P(None, "frames", "chan"),
        P(None, None, "chan"),
        P(None, None, "chan"),
        P(None, None, "chan"),
    )
    return jax.shard_map(body, mesh=mesh, in_specs=in_specs, out_specs=out_specs, check_vma=False)
```

profile of v0, /device:TPU:0, one launch (start us, length us, event | category | flops | bytes accessed | tf_op | source)
XLA Modules:
  0.0 1640.0 jit_solution(5016112764289304104)
XLA Ops:
  12.4 23.1 %all-reduce.33 = (f32[32]{0:T(128)S(1)}, f32[32]{0:T(128)S(1)}) all-reduce(f32[32]{0:T(128)S(1)} %get-tuple-element.160, f32[32]{0:T(128)S(1)} %reduce_sum.180), channel_id=1, replica_groups=mesh['chan'=4,'frames'=8] {'frames'}, use_global_device_ids=true, to_apply=%region_4.5 | all-reduce | flops 64 | bytes 512 | tf_op jit(solution)/shard_map/psum | solution.py:149
  68.2 30.9 %all-gather = bf16[8,160,64]{1,2,0:T(8,128)(2,1)S(1)} all-gather(bf16[1,160,64]{1,2,0:T(8,128)(2,1)S(1)} %convert_bitcast_fusion), channel_id=1, replica_groups=mesh['chan'=4,'frames'=8] {'frames'}, dimensions={0}, use_global_device_ids=true | all-gather | bytes 184320 | tf_op jit(solution)/shard_map/all_gather | solution.py:223
  124.1 26.1 %slice.535 = bf16[336,32,128]{2,1,0:T(8,128)(2,1)} slice(bf16[338,66,128]{2,1,0:T(8,128)(2,1)} %pad.40), slice={[2:338:1], [2:65:2], [0:128:1]} | slice | bytes 5505024 | tf_op jit(solution)/shard_map/slice | solution.py:65
  150.2 25.9 %slice.533 = bf16[336,32,128]{2,1,0:T(8,128)(2,1)} slice(bf16[338,66,128]{2,1,0:T(8,128)(2,1)} %pad.40), slice={[2:338:1], [1:64:2], [0:128:1]} | slice | bytes 5505024 | tf_op jit(solution)/shard_map/slice | solution.py:65
  176.1 25.9 %slice.531 = bf16[336,32,128]{2,1,0:T(8,128)(2,1)} slice(bf16[338,66,128]{2,1,0:T(8,128)(2,1)} %pad.40), slice={[2:338:1], [0:63:2], [0:128:1]} | slice | bytes 5505024 | tf_op jit(solution)/shard_map/slice | solution.py:65
  202.0 23.0 %slice.529 = bf16[336,32,128]{2,1,0:T(8,128)(2,1)S(1)} slice(bf16[338,66,128]{2,1,0:T(8,128)(2,1)} %pad.40), slice={[1:337:1], [2:65:2], [0:128:1]} | slice | bytes 5505024 | tf_op jit(solution)/shard_map/slice | solution.py:65
  225.0 26.0 %slice.527 = bf16[336,32,128]{2,1,0:T(8,128)(2,1)} slice(bf16[338,66,128]{2,1,0:T(8,128)(2,1)} %pad.40), slice={[1:337:1], [1:64:2], [0:128:1]} | slice | bytes 5505024 | tf_op jit(solution)/shard_map/slice | solution.py:65
  251.0 25.9 %slice.525 = bf16[336,32,128]{2,1,0:T(8,128)(2,1)} slice(bf16[338,66,128]{2,1,0:T(8,128)(2,1)} %pad.40), slice={[1:337:1], [0:63:2], [0:128:1]} | slice | bytes 5505024 | tf_op jit(solution)/shard_map/slice | solution.py:65
  276.9 26.0 %slice.521 = bf16[336,32,128]{2,1,0:T(8,128)(2,1)} slice(bf16[338,66,128]{2,1,0:T(8,128)(2,1)} %pad.40), slice={[0:336:1], [2:65:2], [0:128:1]} | slice | bytes 5505024 | tf_op jit(solution)/shard_map/slice | solution.py:65
  303.0 25.9 %slice.519 = bf16[336,32,128]{2,1,0:T(8,128)(2,1)} slice(bf16[338,66,128]{2,1,0:T(8,128)(2,1)} %pad.40), slice={[0:336:1], [1:64:2], [0:128:1]} | slice | bytes 5505024 | tf_op jit(solution)/shard_map/slice | solution.py:65
  328.8 25.9 %slice.516 = bf16[336,32,128]{2,1,0:T(8,128)(2,1)} slice(bf16[338,66,128]{2,1,0:T(8,128)(2,1)} %pad.40), slice={[0:336:1], [0:63:2], [0:128:1]} | slice | bytes 5505024 | tf_op jit(solution)/shard_map/slice | solution.py:65
  400.4 21.3 %all-reduce.32 = (f32[64]{0:T(128)S(1)}, f32[64]{0:T(128)S(1)}) all-reduce(f32[64]{0:T(128)S(1)} %get-tuple-element.123, f32[64]{0:T(128)S(1)} %get-tuple-element.122), channel_id=1, replica_groups=mesh['chan'=4,'frames'=8] {'frames'}, use_global_device_ids=true, to_apply=%region_8.9 | all-reduce | flops 128 | bytes 1024 | tf_op jit(solution)/shard_map/psum | solution.py:149
  456.1 45.3 %all_gather.21 = bf16[3,2304,64]{2,0,1:T(4,128)(2,1)S(1)} all-gather(bf16[3,288,64]{2,0,1:T(4,128)(2,1)S(1)} %copy.730), channel_id=1, replica_groups=mesh['chan'=4,'frames'=8] {'frames'}, dimensions={1}, use_global_device_ids=true | all-gather | bytes 995328 | tf_op jit(solution)/shard_map/all_gather | solution.py:224
  585.4 31.1 %add_convert_fusion.2 = bf16[336,32,256]{2,1,0:T(8,128)(2,1)} fusion(f32[336,31,256]{2,1,0:T(8,128)} %fusion.82, f32[336,31,256]{2,1,0:T(8,128)} %fusion.79, f32[336,31,256]{2,1,0:T(8,128)} %fusion.115, f32[336,32,256]{2,1,0:T(8,128)} %fusion.547, f32[336,31,256]{2,1,0:T(8,128)} %fusion.117, f32[336,31,256]{2,1,0:T(8,128)} %fusion.89, ...), kind=kOutput, calls=%fused_computation.11 | convolution fusion | flops 385359872 | bytes 92936832 | tf_op jit(solution)/shard_map/fbo,io->fbi/dot_general | solution.py:106
  634.9 23.0 %slice.563 = bf16[336,32,128]{2,1,0:T(8,128)(2,1)S(1)} slice(bf16[338,64,128]{2,1,0:T(8,128)(2,1)} %copy.714), slice={[1:337:1], [0:64:2], [0:128:1]} | slice | bytes 5505024 | tf_op jit(solution)/shard_map/slice | solution.py:246
  723.6 20.2 %all-reduce.31 = (f32[64]{0:T(128)S(1)}, f32[64]{0:T(128)S(1)}) all-reduce(f32[64]{0:T(128)S(1)} %get-tuple-element.121, f32[64]{0:T(128)S(1)} %get-tuple-element.120), channel_id=1, replica_groups=mesh['chan'=4,'frames'=8] {'frames'}, use_global_device_ids=true, to_apply=%region_12.13 | all-reduce | flops 128 | bytes 1024 | tf_op jit(solution)/shard_map/psum | solution.py:149
  770.2 34.6 %all-gather.10.cloned.1.call-done = bf16[338,32,256]{0,1,2:T(8,128)(2,1)} async-done(((bf16[338,32,64]{0,1,2:T(8,128)(2,1)}), bf16[338,32,256]{0,1,2:T(8,128)(2,1)}) %all-gather.10.cloned.1.call-update) | async-done | bytes 5537808 | tf_op jit(solution)/shard_map/all_gather | solution.py:40
  869.0 21.4 %all-reduce.30 = (f32[64]{0:T(128)S(1)}, f32[64]{0:T(128)S(1)}) all-reduce(f32[64]{0:T(128)S(1)} %get-tuple-element.119, f32[64]{0:T(128)S(1)} %get-tuple-element.118), channel_id=1, replica_groups=mesh['chan'=4,'frames'=8] {'frames'}, use_global_device_ids=true, to_apply=%region_16.17 | all-reduce | flops 128 | bytes 1024 | tf_op jit(solution)/shard_map/psum | solution.py:149
  970.3 31.1 %add_convert_fusion.1 = bf16[336,32,256]{2,1,0:T(8,128)(2,1)} fusion(f32[336,31,256]{2,1,0:T(8,128)} %fusion.68, f32[336,31,256]{2,1,0:T(8,128)} %fusion.65, f32[336,31,256]{2,1,0:T(8,128)} %fusion.111, f32[336,32,256]{2,1,0:T(8,128)} %fusion.569, f32[336,31,256]{2,1,0:T(8,128)} %fusion.113, f32[336,31,256]{2,1,0:T(8,128)} %fusion.75, ...), kind=kOutput, calls=%fused_computation.10 | convolution fusion | flops 385359872 | bytes 92936832 | tf_op jit(solution)/shard_map/fbo,io->fbi/dot_general | solution.py:106
  1043.1 24.8 %reduce-scatter.11.cloned.1.call-done = bf16[336,32,64]{0,1,2:T(8,128)(2,1)} async-done(((bf16[336,32,256]{0,1,2:T(8,128)(2,1)}), bf16[336,32,64]{0,1,2:T(8,128)(2,1)}) %reduce-scatter.11.cloned.1.call-update) | async-done | bytes 1376272 | tf_op jit(solution)/shard_map/reduce_scatter | solution.py:50
  1081.2 21.3 %all-reduce.28 = (f32[64]{0:T(128)S(1)}, f32[64]{0:T(128)S(1)}) all-reduce(f32[64]{0:T(128)S(1)} %get-tuple-element.115, f32[64]{0:T(128)S(1)} %get-tuple-element.114), channel_id=1, replica_groups=mesh['chan'=4,'frames'=8] {'frames'}, use_global_device_ids=true, to_apply=%region_26.27 | all-reduce | flops 128 | bytes 1024 | tf_op jit(solution)/shard_map/psum | solution.py:168
  1157.1 31.1 %add_convert_fusion = bf16[336,32,256]{2,1,0:T(8,128)(2,1)} fusion(f32[336,31,256]{2,1,0:T(8,128)} %fusion.54, f32[336,31,256]{2,1,0:T(8,128)} %fusion.51, f32[336,31,256]{2,1,0:T(8,128)} %fusion.107, f32[336,32,256]{2,1,0:T(8,128)} %fusion.591, f32[336,31,256]{2,1,0:T(8,128)} %fusion.109, f32[336,31,256]{2,1,0:T(8,128)} %fusion.61, ...), kind=kOutput, calls=%fused_computation.9 | convolution fusion | flops 385359872 | bytes 92936832 | tf_op jit(solution)/shard_map/fbo,io->fbi/dot_general | solution.py:106
  1320.6 20.8 %all-reduce.27 = (f32[64]{0:T(128)S(1)}, f32[64]{0:T(128)S(1)}) all-reduce(f32[64]{0:T(128)S(1)} %get-tuple-element.113, f32[64]{0:T(128)S(1)} %get-tuple-element.112), channel_id=1, replica_groups=mesh['chan'=4,'frames'=8] {'frames'}, use_global_device_ids=true, to_apply=%region_31.32 | all-reduce | flops 128 | bytes 1024 | tf_op jit(solution)/shard_map/psum | solution.py:168
  1589.3 36.8 %psum.135 = f32[]{:T(128)} all-reduce(f32[]{:T(128)S(6)} %add.588), channel_id=1, replica_groups=mesh['chan'=4,'frames'=8] {'chan','frames'}, use_global_device_ids=true, to_apply=%region_42.43 | all-reduce | flops 1 | bytes 8 | tf_op jit(solution)/shard_map/psum | solution.py:329
  (689 shorter events, 971.8 us)
Async XLA Ops:
  7.2 99.2 %all-gather.6.cloned.1.call-start = ((), (), s32[]{:S(2)}) async-start(), calls=%async_computation.6 | async-start | bytes 7864320 | tf_op jit(solution)/shard_map/all_gather | solution.py:40
  37.8 20.2 %collective-permute-start = (bf16[1,64,32]{0,1,2:T(8,128)(2,1)S(1)}, bf16[1,64,32]{0,1,2:T(8,128)(2,1)S(1)}, u32[]{:S(2)}, u32[]{:S(2)}) collective-permute-start(bf16[1,64,32]{0,1,2:T(8,128)(2,1)S(1)} %get-tuple-element.178), channel_id=1, source_target_pairs={{0,1},{1,2},{2,3},{3,4},{4,5},{5,6},{6,7},{8,9},{9,10},{10,11},{11... | collective-permute-start | bytes 12296 | tf_op jit(solution)/shard_map/ppermute | solution.py:26
  39.2 18.9 %collective-permute-start.1 = (bf16[1,64,32]{0,1,2:T(8,128)(2,1)S(1)}, bf16[1,64,32]{0,1,2:T(8,128)(2,1)S(1)}, u32[]{:S(2)}, u32[]{:S(2)}) collective-permute-start(bf16[1,64,32]{0,1,2:T(8,128)(2,1)S(1)} %get-tuple-element.179), channel_id=1, source_target_pairs={{1,0},{2,1},{3,2},{4,3},{5,4},{6,5},{7,6},{9,8},{10,9},{11,10},{12... | collective-permute-start | bytes 12296 | tf_op jit(solution)/shard_map/ppermute | solution.py:29
  60.4 600.8 %all-gather.8.cloned.1.call-start = ((), (), s32[]{:S(2)}) async-start(), calls=%async_computation.7 | async-start | bytes 7864320 | tf_op jit(solution)/shard_map/all_gather | solution.py:40
  61.0 40.4 %collective-permute-start.2 = (s32[1]{0:T(128)}, s32[1]{0:T(128)}, u32[]{:S(2)}, u32[]{:S(2)}) collective-permute-start(s32[1]{0:T(128)} %get-tuple-element.231), channel_id=1, source_target_pairs={{0,1},{1,2},{2,3},{3,4},{4,5},{5,6},{6,7},{8,9},{9,10},{10,11},{11... | collective-permute-start | bytes 20 | tf_op jit(solution)/shard_map/ppermute | solution.py:26
  65.9 35.5 %collective-permute-start.3 = (s32[1]{0:T(128)}, s32[1]{0:T(128)}, u32[]{:S(2)}, u32[]{:S(2)}) collective-permute-start(s32[1]{0:T(128)} %get-tuple-element.232), channel_id=1, source_target_pairs={{1,0},{2,1},{3,2},{4,3},{5,4},{6,5},{7,6},{9,8},{10,9},{11,10},{12... | collective-permute-start | bytes 20 | tf_op jit(solution)/shard_map/ppermute | solution.py:29
  439.4 324.0 %reduce-scatter.9.cloned.1.call-start = ((), (), s32[]{:S(2)}) async-start(), calls=%async_computation.10 | async-start | bytes 7864320 | tf_op jit(solution)/shard_map/reduce_scatter | solution.py:50
  449.4 104.0 %collective-permute-start.10 = (bf16[1,32,64]{2,1,0:T(8,128)(2,1)}, bf16[1,32,64]{2,1,0:T(8,128)(2,1)}, u32[]{:S(2)}, u32[]{:S(2)}) collective-permute-start(bf16[1,32,64]{2,1,0:T(8,128)(2,1)} %get-tuple-element.170), channel_id=1, source_target_pairs={{1,0},{2,1},{3,2},{4,3},{5,4},{6,5},{7,6},{9,8},{10,9},{11,10},{12... | collective-permute-start | bytes 12296 | tf_op jit(solution)/shard_map/ppermute | solution.py:29
  450.7 121.7 %collective-permute-start.11 = (bf16[1,32,64]{2,1,0:T(8,128)(2,1)}, bf16[1,32,64]{2,1,0:T(8,128)(2,1)}, u32[]{:S(2)}, u32[]{:S(2)}) collective-permute-start(bf16[1,32,64]{2,1,0:T(8,128)(2,1)} %get-tuple-element.171), channel_id=1, source_target_pairs={{0,1},{1,2},{2,3},{3,4},{4,5},{5,6},{6,7},{8,9},{9,10},{10,11},{11... | collective-permute-start | bytes 12296 | tf_op jit(solution)/shard_map/ppermute | solution.py:26
  626.1 178.7 %all-gather.10.cloned.1.call-start = ((), (), s32[]{:S(2)}) async-start(), calls=%async_computation.8 | async-start | bytes 7864320 | tf_op jit(solution)/shard_map/all_gather | solution.py:40
  760.7 307.2 %reduce-scatter.11.cloned.1.call-start = ((), (), s32[]{:S(2)}) async-start(), calls=%async_computation.11 | async-start | bytes 7864320 | tf_op jit(solution)/shard_map/reduce_scatter | solution.py:50
  931.2 11.0 collective-permute-start.13
  940.7 12.7 collective-permute-start.12
  1011.0 200.1 %all-gather.12.cloned.1.call-start = ((), (), s32[]{:S(2)}) async-start(), calls=%async_computation.9 | async-start | bytes 7864320 | tf_op jit(solution)/shard_map/all_gather | solution.py:40
  1011.9 24.7 %collective-permute-start.8 = (bf16[1,32,64]{2,1,0:T(8,128)(2,1)S(1)}, bf16[1,32,64]{2,1,0:T(8,128)(2,1)S(1)}, u32[]{:S(2)}, u32[]{:S(2)}) collective-permute-start(bf16[1,32,64]{2,1,0:T(8,128)(2,1)S(1)} %get-tuple-element.172), channel_id=1, source_target_pairs={{0,1},{1,2},{2,3},{3,4},{4,5},{5,6},{6,7},{8,9},{9,10},{10,11},{11... | collective-permute-start | bytes 12296 | tf_op jit(solution)/shard_map/ppermute | solution.py:26
  1016.4 20.2 %collective-permute-start.9 = (bf16[1,32,64]{2,1,0:T(8,128)(2,1)S(1)}, bf16[1,32,64]{2,1,0:T(8,128)(2,1)S(1)}, u32[]{:S(2)}, u32[]{:S(2)}) collective-permute-start(bf16[1,32,64]{2,1,0:T(8,128)(2,1)S(1)} %get-tuple-element.173), channel_id=1, source_target_pairs={{1,0},{2,1},{3,2},{4,3},{5,4},{6,5},{7,6},{9,8},{10,9},{11,10},{12... | collective-permute-start | bytes 12296 | tf_op jit(solution)/shard_map/ppermute | solution.py:29
  1043.1 264.6 %reduce-scatter.13.cloned.1.call-start = ((), (), s32[]{:S(2)}) async-start(), calls=%async_computation.12 | async-start | bytes 7864320 | tf_op jit(solution)/shard_map/reduce_scatter | solution.py:50
  1109.2 19.8 %collective-permute-start.15 = (bf16[1,32,64]{2,1,0:T(8,128)(2,1)S(1)}, bf16[1,32,64]{2,1,0:T(8,128)(2,1)S(1)}, u32[]{:S(2)}, u32[]{:S(2)}) collective-permute-start(bf16[1,32,64]{2,1,0:T(8,128)(2,1)S(1)} %get-tuple-element.167), channel_id=1, source_target_pairs={{0,1},{1,2},{2,3},{3,4},{4,5},{5,6},{6,7},{8,9},{9,10},{10,11},{11... | collective-permute-start | bytes 12296 | tf_op jit(solution)/shard_map/ppermute | solution.py:26
  1127.3 12.9 collective-permute-start.14
  1197.8 352.6 %reduce-scatter.19.cloned.1.call-start = ((), (), s32[]{:S(2)}) async-start(), calls=%async_computation.15 | async-start | bytes 1327104
  1307.6 246.2 %reduce-scatter.17.cloned.1.call-start = ((), (), s32[]{:S(2)}) async-start(), calls=%async_computation.14 | async-start | bytes 368640 | tf_op jit(solution)/shard_map/reduce_scatter | solution.py:312
  1360.3 63.7 %collective-permute-start.16 = (bf16[1,32,64]{2,1,0:T(8,128)(2,1)S(1)}, bf16[1,32,64]{2,1,0:T(8,128)(2,1)S(1)}, u32[]{:S(2)}, u32[]{:S(2)}) collective-permute-start(bf16[1,32,64]{2,1,0:T(8,128)(2,1)S(1)} %get-tuple-element.164), channel_id=1, source_target_pairs={{1,0},{2,1},{3,2},{4,3},{5,4},{6,5},{7,6},{9,8},{10,9},{11,10},{12... | collective-permute-start | bytes 12296 | tf_op jit(solution)/shard_map/ppermute | solution.py:29
  1361.6 34.8 %collective-permute-start.17 = (bf16[1,32,64]{2,1,0:T(8,128)(2,1)S(1)}, bf16[1,32,64]{2,1,0:T(8,128)(2,1)S(1)}, u32[]{:S(2)}, u32[]{:S(2)}) collective-permute-start(bf16[1,32,64]{2,1,0:T(8,128)(2,1)S(1)} %get-tuple-element.165), channel_id=1, source_target_pairs={{0,1},{1,2},{2,3},{3,4},{4,5},{5,6},{6,7},{8,9},{9,10},{10,11},{11... | collective-permute-start | bytes 12296 | tf_op jit(solution)/shard_map/ppermute | solution.py:26
  1396.0 160.5 %reduce-scatter.15.cloned.1.call-start = ((), (), s32[]{:S(2)}) async-start(), calls=%async_computation.13 | async-start | bytes 7864320 | tf_op jit(solution)/shard_map/reduce_scatter | solution.py:50
  (168 other events, 6606.1 us)
Sparse Core Ops, SparseCore 0:
  60.5 45.8 all-gather.5
  439.5 43.8 all-gather.7
  626.2 57.1 reduce-scatter.8
  760.9 43.9 all-gather.9
  1011.2 56.7 reduce-scatter.10
  1069.4 46.3 all-gather.11
  1197.9 57.1 reduce-scatter.12
  1307.7 63.5 reduce-scatter.18
  1396.1 57.1 reduce-scatter.16
  1479.9 54.2 reduce-scatter.14
where the time goes:
time: 1660 us; the launch traced here: 1640 us
  matrix products  556 us (33%)
  local copies, waits for them, and re-layouts  543 us (33%)
  blocking collectives  275 us (17%)
  other arithmetic  114 us (7%)
  waiting for transfers between devices  88.4 us (5%)
  starting transfers between devices  42.2 us (3%)
  between operations  20.8 us (1%)
    dot_general x36, matrix products, conv_grad_input(): jnp.einsum('fbo,io->fbi', rows_used, taps[:, 3 * time_tap + freq_tap], pr...  250 us
    slice x9, local copies, waits for them, and re-layouts, conv_local(): widened[time_tap:time_tap + frames, freq_tap:freq_tap + stride * (out_bin...  231 us
    dot_general x36, matrix products, conv_local(): jnp.einsum('fbi,io->fbo', window, taps[:, 3 * time_tap + freq_tap], prefe...  208 us
    dot_general x36, matrix products, conv_grad_weight(): jnp.einsum('fbi,fbo->io', window, weighted[time_tap], preferred_element_t...  88.8 us
    psum x4, blocking collectives, statistics(): lax.psum((jnp.sum(values, axis=(0, 1)), jnp.sum(values * values, axis=(0,...  86 us
    psum x4, blocking collectives, norm_backward(): lax.psum((jnp.sum(pre_grad, axis=(0, 1)), jnp.sum(pre_grad * scaled, axis...  76.4 us
    unnamed x381, local copies, waits for them, and re-layouts  61.5 us
    all_gather x1, blocking collectives, body(): lax.all_gather(wide_weight.astype(jnp.bfloat16), 'frames', axis=1, tiled=...  45.3 us
  transfers between devices with their start and end apart: 28, of which 6 were waited for; matrix products, arithmetic and copies ran while one was open for 45% of the time, Pallas kernels for 0%

commit v1 on v0

v1 whole, which is shorter than its diff:
```python
import functools

import jax
import jax.numpy as jnp
import numpy as np
from jax import lax
from jax.experimental import pallas as pl
from jax.experimental.pallas import tpu as pltpu
from jax.sharding import PartitionSpec as P

B0 = 64
STEP = 10
B1 = 32
HALO = 6

norm_epsilon = 1e-05
clip_limit = 100.0
beta_first = 0.9
beta_second = 0.999
adam_epsilon = 1e-08
conv_rate = 0.05
norm_rate = 0.5
weight_decay = 0.01

BOTH = ("chan", "frames")
VMEM_BYTES = 56 * 1024 * 1024
F32 = jnp.float32
BF16 = jnp.bfloat16


def total_sum(vector):
    count = lax.axis_size("chan") * lax.axis_size("frames")
    copies = jnp.broadcast_to(vector[None], (count,) + vector.shape)
    return jnp.sum(lax.all_to_all(copies, BOTH, 0, 0, tiled=True), axis=0)


def frame_edges(block, width):
    count = lax.axis_size("frames")
    forward = [(i, i + 1) for i in range(count - 1)]
    backward = [(b, a) for a, b in forward]
    low = lax.ppermute(block[block.shape[0] - width :], "frames", forward)
    high = lax.ppermute(block[:width], "frames", backward)
    return jnp.concatenate([low, block, high], axis=0)


def to_frames(block):
    parts = lax.axis_size("chan")
    own = block.shape[0] // parts
    padded = frame_edges(block, HALO)
    windows = jnp.stack([padded[k * own : k * own + own + 2 * HALO] for k in range(parts)])
    return lax.all_to_all(windows, "chan", 0, 0, tiled=True)


def halves(axis):
    step = lax.axis_size(axis) // 2
    steps = []
    while step:
        steps.append(step)
        step //= 2
    return steps


def scatter_sum(block, axis):
    size = lax.axis_size(axis)
    for step in halves(axis):
        half = block.shape[0] // 2
        mine = (lax.axis_index(axis) // step) % 2
        send = lax.dynamic_slice_in_dim(block, (1 - mine) * half, half, 0)
        keep = lax.dynamic_slice_in_dim(block, mine * half, half, 0)
        came = lax.ppermute(send, axis, [(i, i ^ step) for i in range(size)])
        block = (keep.astype(F32) + came.astype(F32)).astype(BF16)
    return block


def sigmoid(z):
    return 1.0 / (1.0 + jnp.exp(-z))


def shifts(flat):
    rows = flat.shape[0]
    bins = lax.broadcasted_iota(jnp.int32, flat.shape, 0) % B1
    below = jnp.where(bins == 0, 0.0, pltpu.roll(flat, 1, 0))
    above = jnp.where(bins == B1 - 1, 0.0, pltpu.roll(flat, rows - 1, 0))
    return below, above


def fit(count, target, unit=1):
    return max([k for k in range(unit, target + 1, unit) if count % k == 0], default=count)


def loop(low, high, target, body, unit=1):
    chunk = fit(high - low, target, unit)

    def step(i, carry):
        body(low + i * chunk, chunk)
        return carry

    if chunk == high - low:
        body(low, chunk)
    else:
        lax.fori_loop(0, (high - low) // chunk, step, 0)


def mask_frames(partial, mask_ref, base, chunk):
    cube = partial.reshape(chunk, B1, partial.shape[-1])
    return jnp.concatenate([cube[k] * mask_ref[base + k] for k in range(chunk)], axis=0)


def taps_sum(cols_ref, taps_ref, masks, base, chunk):
    total = None
    for tap in (1, 0, 2):
        rows = cols_ref[pl.ds(base + tap - 1, chunk)].reshape(chunk * B1, cols_ref.shape[-1])
        partial = jnp.dot(rows, taps_ref[tap], preferred_element_type=F32)
        if tap == 0:
            partial = mask_frames(partial, masks[0], base, chunk)
        if tap == 2:
            partial = mask_frames(partial, masks[1], base, chunk)
        total = partial if total is None else total + partial
    return total


def own_rows(value, base, chunk, low, high):
    frame = base + lax.broadcasted_iota(jnp.int32, value.shape, 0) // B1
    return jnp.where((frame >= low) & (frame < high), value, 0.0)


def add_sums(sums_ref, first, second):
    rows, channels = first.shape
    sums_ref[0] += jnp.sum(first.reshape(rows // 8, 8, channels), axis=0)
    sums_ref[1] += jnp.sum(second.reshape(rows // 8, 8, channels), axis=0)


def rows_of(ref, base, chunk):
    return ref[pl.ds(base, chunk)].reshape(chunk * B1, ref.shape[-1])


def put(ref, base, chunk, value):
    ref[pl.ds(base, chunk)] = value.reshape(chunk, B1, value.shape[-1]).astype(ref.dtype)


def normal(values, vec_ref):
    return (values - vec_ref[0:1]) * vec_ref[1:2]


def transposed(rows):
    channels = rows.shape[1]
    eye = (
        lax.broadcasted_iota(jnp.int32, (channels, channels), 0)
        == lax.broadcasted_iota(jnp.int32, (channels, channels), 1)
    ).astype(BF16)
    return lax.dot_general(
        eye, rows, (((1,), (1,)), ((), ())), preferred_element_type=F32
    ).astype(BF16)


def first_kernel(own, prev_ref, next_ref, x_ref, vec_ref, taps_ref, short_ref, h_ref, s_ref, a_ref, sums_ref, cols_ref):
    total = x_ref.shape[1]

    def build(base, chunk):
        acts = []
        for parity in range(2):
            flat = rows_of(x_ref.at[parity], base, chunk).astype(F32)
            z = normal(flat, vec_ref) * vec_ref[2:3] + vec_ref[3:4]
            act = z * sigmoid(z)
            put(a_ref.at[parity], base, chunk, act)
            acts.append(act)
        below, _ = shifts(acts[1])
        put(cols_ref, base, chunk, jnp.concatenate([below, acts[0], acts[1]], axis=1))

    loop(0, total, 8, build)
    sums_ref[...] = jnp.zeros_like(sums_ref)

    def conv(base, chunk):
        result = taps_sum(cols_ref, taps_ref, (prev_ref, next_ref), base, chunk)
        put(h_ref, base, chunk, result)
        mine = own_rows(result, base, chunk, HALO, HALO + own)
        add_sums(sums_ref, mine, mine * mine)
        short = jnp.dot(rows_of(a_ref.at[0], base, chunk), short_ref[...], preferred_element_type=F32)
        put(s_ref, base, chunk, short)

    loop(1, total - 1, 47, conv)


def forward_kernel(own, lead, chunk, with_short, prev_ref, next_ref, h_ref, vec_ref, taps_ref, *rest):
    if with_short:
        s_ref, out_ref, a_ref, sums_ref, cols_ref = rest
    else:
        out_ref, a_ref, sums_ref, cols_ref = rest
    total = h_ref.shape[0]
    activate_into(h_ref, vec_ref, a_ref, cols_ref, lead - 1)
    sums_ref[...] = jnp.zeros_like(sums_ref)

    def conv(base, chunk):
        result = taps_sum(cols_ref, taps_ref, (prev_ref, next_ref), base, chunk)
        if with_short:
            result = result + rows_of(s_ref, base, chunk)
        put(out_ref, base, chunk, result)
        mine = own_rows(result, base, chunk, HALO, HALO + own)
        add_sums(sums_ref, mine, mine * mine)

    loop(lead, total - lead, chunk, conv)


def activate_into(h_ref, vec_ref, a_ref, cols_ref, lead):
    total = h_ref.shape[0]

    def build(base, chunk):
        flat = rows_of(h_ref, base, chunk)
        z = normal(flat, vec_ref) * vec_ref[2:3] + vec_ref[3:4]
        act = z * sigmoid(z)
        put(a_ref, base, chunk, act)
        below, above = shifts(act)
        put(cols_ref, base, chunk, jnp.concatenate([below, act, above], axis=1))

    loop(lead, total - lead, 2, build)


def back_through(q, values, vec_ref):
    xhat = normal(values, vec_ref)
    z = xhat * vec_ref[2:3] + vec_ref[3:4]
    gate = sigmoid(z)
    return q * gate * (1.0 + z * (1.0 - gate)), xhat


def weight_grad(own, u_ref, cols_ref, masks, out_ref, turned_ref):
    rows = own * B1
    for tap in range(3):
        def turn(base, chunk):
            u = u_ref[pl.ds(HALO + base, chunk)].reshape(chunk * B1, u_ref.shape[-1])
            if tap != 1:
                u = mask_frames(u.astype(F32), masks[0 if tap == 0 else 1], HALO + base, chunk).astype(BF16)
            turned_ref[:, pl.ds(pl.multiple_of(base * B1, chunk * B1), chunk * B1)] = transposed(u)

        loop(0, own, 12, turn, 4)
        other = cols_ref[pl.ds(HALO + 1 - tap, own)].reshape(rows, cols_ref.shape[-1])
        out_ref[tap] = jnp.dot(turned_ref[...], other, preferred_element_type=F32).astype(out_ref.dtype)


def shift_into(value, base, chunk, cols_ref):
    below, above = shifts(value)
    put(cols_ref, base, chunk, jnp.concatenate([above, value, below], axis=1))


def last_kernel(
    own, prev_ref, next_ref, h_ref, x_ref, e_ref, vec_ref, taps_ref, turned_taps_ref,
    y_ref, dz_ref, sums_ref, grad_ref, cols_ref, a_ref, turned_ref,
):
    total = h_ref.shape[0]
    activate_into(h_ref, vec_ref, a_ref, cols_ref, 3)

    def conv(base, chunk):
        result = taps_sum(cols_ref, taps_ref, (prev_ref, next_ref), base, chunk) + rows_of(x_ref, base, chunk)
        put(y_ref, base - HALO, chunk, result)

    loop(HALO, HALO + own, 12, conv)

    def build(base, chunk):
        shift_into(rows_of(e_ref, base, chunk).astype(F32), base, chunk, cols_ref)

    loop(2, total - 2, 2, build)
    sums_ref[...] = jnp.zeros_like(sums_ref)

    def back(base, chunk):
        q = taps_sum(cols_ref, turned_taps_ref, (prev_ref, next_ref), base, chunk)
        dz, xhat = back_through(q, rows_of(h_ref, base, chunk), vec_ref)
        put(dz_ref, base, chunk, dz)
        mine = own_rows(dz, base, chunk, HALO, HALO + own)
        add_sums(sums_ref, mine, mine * xhat)

    loop(3, total - 3, 15, back)
    weight_grad(own, a_ref, cols_ref, (next_ref, prev_ref), grad_ref, turned_ref)


def middle_kernel(
    own, lead, chunk, with_top, prev_ref, next_ref, dz_ref, h_ref, low_ref, u_ref, vec_ref, coef_ref, low_vec_ref, turned_taps_ref, *rest,
):
    if with_top:
        e_ref, even_ref, dz_out_ref, sums_ref, grad_ref, short_ref, e1_ref, cols_ref, turned_ref = rest
    else:
        dz_out_ref, sums_ref, grad_ref, cols_ref, turned_ref = rest
    total = h_ref.shape[0]

    def build(base, size):
        xhat = normal(rows_of(h_ref, base, size), vec_ref)
        d = vec_ref[2:3] * vec_ref[1:2] * (rows_of(dz_ref, base, size) - coef_ref[0:1] - xhat * coef_ref[1:2])
        if with_top:
            d = d + rows_of(e_ref, base, size).astype(F32)
            put(e1_ref, base, size, d)
        shift_into(d, base, size, cols_ref)

    loop(lead - 1, total - lead + 1, 2, build)
    sums_ref[...] = jnp.zeros_like(sums_ref)

    def back(base, chunk):
        q = taps_sum(cols_ref, turned_taps_ref, (prev_ref, next_ref), base, chunk)
        dz, xhat = back_through(q, rows_of(low_ref, base, chunk), low_vec_ref)
        put(dz_out_ref, base, chunk, dz)
        mine = own_rows(dz, base, chunk, HALO, HALO + own)
        add_sums(sums_ref, mine, mine * xhat)

    loop(lead, total - lead, chunk, back)
    weight_grad(own, u_ref, cols_ref, (next_ref, prev_ref), grad_ref, turned_ref)
    if with_top:
        rows = own * B1
        def turn(base, size):
            u = even_ref[pl.ds(HALO + base, size)].reshape(size * B1, even_ref.shape[-1])
            turned_ref[0 : even_ref.shape[-1], pl.ds(pl.multiple_of(base * B1, size * B1), size * B1)] = transposed(u)

        loop(0, own, 12, turn, 4)
        short_ref[...] = jnp.dot(
            turned_ref[0 : even_ref.shape[-1]],
            e1_ref[pl.ds(HALO, own)].reshape(rows, e1_ref.shape[-1]),
            preferred_element_type=F32,
        ).astype(BF16)


def bottom_kernel(
    own, prev_ref, next_ref, dz_ref, h_ref, x_ref, a_ref, e1_ref, vec_ref, coef_ref, low_vec_ref, turned_taps_ref, turned_short_ref,
    dz_out_ref, sums_ref, grad_ref, cols_ref, turned_ref,
):
    total = h_ref.shape[0]

    def build(base, size):
        xhat = normal(rows_of(h_ref, base, size), vec_ref)
        d = vec_ref[2:3] * vec_ref[1:2] * (rows_of(dz_ref, base, size) - coef_ref[0:1] - xhat * coef_ref[1:2])
        _, above = shifts(d)
        put(cols_ref, base, size, jnp.concatenate([d, above], axis=1))

    loop(HALO - 1, total - HALO + 1, 2, build)
    sums_ref[...] = jnp.zeros_like(sums_ref)
    half = x_ref.shape[-1]

    def back(base, chunk):
        q = taps_sum(cols_ref, turned_taps_ref, (prev_ref, next_ref), base, chunk)
        r = jnp.dot(rows_of(e1_ref, base, chunk), turned_short_ref[...], preferred_element_type=F32)
        parts = (q[:, :half] + r, q[:, half:])
        for parity in range(2):
            dz, xhat = back_through(parts[parity], rows_of(x_ref.at[parity], base, chunk).astype(F32), low_vec_ref)
            put(dz_out_ref.at[parity], base - HALO, chunk, dz)
            add_sums(sums_ref, dz, dz * xhat)

    loop(HALO, HALO + own, 12, back)
    rows = own * B1
    for tap in range(3):
        def turn(base, chunk):
            for parity in range(2):
                u = a_ref[parity, pl.ds(HALO + base, chunk)].reshape(chunk * B1, half)
                if tap != 1:
                    u = mask_frames(u.astype(F32), next_ref if tap == 0 else prev_ref, HALO + base, chunk).astype(BF16)
                turned_ref[parity * half : parity * half + half, pl.ds(pl.multiple_of(base * B1, chunk * B1), chunk * B1)] = transposed(u)

        loop(0, own, 12, turn, 4)
        other = cols_ref[pl.ds(HALO + 1 - tap, own)].reshape(rows, cols_ref.shape[-1])
        grad_ref[tap] = jnp.dot(turned_ref[...], other, preferred_element_type=F32).astype(grad_ref.dtype)


def input_kernel(own, dz_ref, x_ref, vec_ref, coef_ref, g_ref):
    def build(base, chunk):
        for parity in range(2):
            xhat = normal(rows_of(x_ref.at[parity], HALO + base, chunk).astype(F32), vec_ref)
            dz = rows_of(dz_ref.at[parity], base, chunk)
            g = vec_ref[2:3] * vec_ref[1:2] * (dz - coef_ref[0:1] - xhat * coef_ref[1:2])
            put(g_ref.at[parity], base, chunk, g)

    loop(0, own, 4, build)


SMEM = pl.BlockSpec(memory_space=pltpu.SMEM)
VMEM = pl.BlockSpec(memory_space=pltpu.VMEM)


def run(kernel, masks, operands, outs, scratch):
    return pl.pallas_call(
        kernel,
        in_specs=[SMEM] * len(masks) + [VMEM] * len(operands),
        out_specs=[VMEM] * len(outs),
        out_shape=[jax.ShapeDtypeStruct(shape, kind) for shape, kind in outs],
        scratch_shapes=[pltpu.VMEM(shape, kind) for shape, kind in scratch],
        compiler_params=pltpu.CompilerParams(vmem_limit_bytes=VMEM_BYTES),
    )(*masks, *operands)


def norm_pair(params, norm_index):
    if norm_index == 0:
        return (params[0, 0], params[1, 0])
    row_pair = params[:, 2 * norm_index - 1 : 2 * norm_index + 1]
    packed = jnp.transpose(row_pair, (0, 2, 1)).reshape(2, -1)
    return (packed[0], packed[1])


def pack_norms(vectors):
    blocks = [vectors[0][None]]
    for vector in vectors[1:]:
        blocks.append(vector.reshape(-1, 2).T)
    return jnp.concatenate(blocks, axis=0)


def adam_step(weight, moment, square, gradient, step_rate, decay_rate):
    moment_next = beta_first * moment + (1.0 - beta_first) * gradient
    square_next = beta_second * square + (1.0 - beta_second) * gradient * gradient
    corrected = moment_next / (1.0 - beta_first**STEP)
    divisor = jnp.sqrt(square_next / (1.0 - beta_second**STEP)) + adam_epsilon
    weight_next = weight - step_rate * (corrected / divisor + decay_rate * weight)
    return (weight_next, moment_next, square_next)


def vectors(sums, count, pair):
    average = sums[0] / count
    spread = lax.rsqrt(sums[1] / count - average * average + norm_epsilon)
    return jnp.stack([average, spread, pair[0], pair[1]])


def body(
    signal,
    clip_ids,
    output_grad,
    first_weight,
    first_mean,
    first_square,
    wide_weight,
    wide_mean,
    wide_square,
    norm_params,
    norm_mean,
    norm_square,
):
    chan_count = lax.axis_size("chan")
    frame_count = lax.axis_size("frames")
    chan = lax.axis_index("chan")
    group = signal.shape[0]
    own = group // chan_count
    total = own + 2 * HALO
    frames = group * frame_count
    in_local = signal.shape[1] // B0
    in_channels = in_local * chan_count
    wide_local = output_grad.shape[1] // B1
    wide = wide_local * chan_count

    ids = frame_edges(clip_ids + 1, HALO + 1)
    ids = lax.dynamic_slice_in_dim(ids, chan * own, total + 2, 0)
    prev_mask = (ids[:-2] == ids[1:-1]).astype(F32)
    next_mask = (ids[2:] == ids[1:-1]).astype(F32)
    masks = (prev_mask, next_mask)

    local = signal.astype(F32).reshape(group, in_local, B0)
    local_sums = jnp.stack([jnp.sum(local, axis=(0, 2)), jnp.sum(local * local, axis=(0, 2))])
    placed = lax.dynamic_update_slice(jnp.zeros((2, in_channels), F32), local_sums, (0, chan * in_local))
    sums_zero = total_sum(placed)

    came = to_frames(signal).reshape(chan_count, total, in_local, B1, 2)
    x_zero = jnp.transpose(came, (4, 1, 3, 0, 2)).reshape(2, total, B1, in_channels)
    came = to_frames(output_grad).reshape(chan_count, total, wide_local, B1)
    top = jnp.transpose(came, (1, 3, 0, 2)).reshape(total, B1, wide)

    columns = first_weight.shape[1]
    first_all = lax.all_gather(first_weight.astype(BF16), ("frames", "chan"), axis=0)
    first_all = first_all.reshape(frame_count, chan_count, -1, columns)
    first_all = jnp.transpose(first_all, (0, 2, 1, 3)).reshape(-1, chan_count * columns)
    wide_all = lax.all_gather(wide_weight.astype(BF16), ("frames", "chan"), axis=0)
    wide_all = wide_all.reshape(frame_count, chan_count, 3, -1, 9, columns)
    wide_all = jnp.transpose(wide_all, (2, 4, 0, 3, 1, 5)).reshape(3, 9, wide, wide)
    first_taps = jnp.transpose(first_all[: 9 * in_channels].reshape(in_channels, 9, wide), (1, 0, 2))
    short_taps = first_all[9 * in_channels :]
    taps_one = first_taps.reshape(3, 3 * in_channels, wide)
    taps = [wide_all[k].reshape(3, 3 * wide, wide) for k in range(3)]
    turned = jnp.transpose(wide_all, (0, 1, 3, 2)).reshape(3, 3, 3, wide, wide)
    turned = [turned[k][::-1].reshape(3, 3 * wide, wide) for k in range(3)]
    back_first = jnp.transpose(first_taps, (0, 2, 1)).reshape(3, 3, wide, in_channels)[::-1]
    turned_one = jnp.concatenate(
        [
            jnp.concatenate([back_first[:, 1], back_first[:, 2]], axis=2),
            jnp.concatenate([jnp.zeros_like(back_first[:, 0]), back_first[:, 0]], axis=2),
        ],
        axis=1,
    )
    turned_short = short_taps.T

    params = lax.all_gather(norm_params, "chan", axis=2, tiled=True)
    pairs = [norm_pair(params, k) for k in range(4)]

    count_zero = frames * B0
    count = frames * B1
    cube = (total, B1, wide)
    cols = (total, B1, 3 * wide)
    turned_shape = (wide, own * B1)

    def gathered(sums):
        return total_sum(jnp.sum(sums, axis=1))

    vec_zero = vectors(sums_zero, count_zero, pairs[0])
    hidden_one, shortcut, act_one, sums = run(
        functools.partial(first_kernel, own),
        masks,
        (x_zero, vec_zero, taps_one, short_taps),
        [(cube, F32), (cube, F32), ((2, total, B1, in_channels), BF16), ((2, 8, wide), F32)],
        [((total, B1, 3 * in_channels), BF16)],
    )
    vec_one = vectors(gathered(sums), count, pairs[1])
    residual, mid_one, sums = run(
        functools.partial(forward_kernel, own, 2, 23, True),
        masks,
        (hidden_one, vec_one, taps[0], shortcut),
        [(cube, F32), (cube, BF16), ((2, 8, wide), F32)],
        [(cols, BF16)],
    )
    vec_two = vectors(gathered(sums), count, pairs[2])
    hidden_two, act_two, sums = run(
        functools.partial(forward_kernel, own, 3, 15, False),
        masks,
        (residual, vec_two, taps[1]),
        [(cube, F32), (cube, BF16), ((2, 8, wide), F32)],
        [(cols, BF16)],
    )
    vec_three = vectors(gathered(sums), count, pairs[3])
    block_cube, dz_three, sums_three, grad_four = run(
        functools.partial(last_kernel, own),
        masks,
        (hidden_two, residual, top, vec_three, taps[2], turned[2]),
        [((own, B1, wide), BF16), (cube, F32), ((2, 8, wide), F32), ((3, wide, 3 * wide), BF16)],
        [(cols, BF16), (cube, BF16), (turned_shape, BF16)],
    )
    norm_three = gathered(sums_three)
    dz_two, sums_two, grad_three = run(
        functools.partial(middle_kernel, own, 4, 11, False),
        masks,
        (dz_three, hidden_two, residual, act_two, vec_three, norm_three / count, vec_two, turned[1]),
        [(cube, F32), ((2, 8, wide), F32), ((3, wide, 3 * wide), BF16)],
        [(cols, BF16), (turned_shape, BF16)],
    )
    norm_two = gathered(sums_two)
    dz_one, sums_one, grad_two, grad_short, low_top = run(
        functools.partial(middle_kernel, own, 5, 43, True),
        masks,
        (dz_two, residual, hidden_one, mid_one, vec_two, norm_two / count, vec_one, turned[0], top, act_one[0]),
        [(cube, F32), ((2, 8, wide), F32), ((3, wide, 3 * wide), BF16), ((in_channels, wide), BF16), (cube, BF16)],
        [(cols, BF16), (turned_shape, BF16)],
    )
    norm_one = gathered(sums_one)
    dz_zero, sums_last, grad_one = run(
        functools.partial(bottom_kernel, own),
        masks,
        (dz_one, hidden_one, x_zero, act_one, low_top, vec_one, norm_one / count, vec_zero, turned_one, turned_short),
        [((2, own, B1, in_channels), F32), ((2, 8, in_channels), F32), ((3, 2 * in_channels, 2 * wide), BF16)],
        [((total, B1, 2 * wide), BF16), ((2 * in_channels, own * B1), BF16)],
    )
    norm_zero = gathered(sums_last)
    (input_cube,) = run(
        functools.partial(input_kernel, own),
        (),
        (dz_zero, x_zero, vec_zero, norm_zero / count_zero),
        [((2, own, B1, in_channels), BF16)],
        [],
    )

    out = jnp.transpose(block_cube.reshape(own, B1, chan_count, wide_local), (2, 0, 3, 1))
    out = lax.all_to_all(out.reshape(chan_count, own, wide_local * B1), "chan", 0, 0, tiled=True)
    block_out = out.reshape(group, -1).astype(F32)
    out = jnp.transpose(input_cube.reshape(2, own, B1, chan_count, in_local), (3, 1, 4, 2, 0))
    out = lax.all_to_all(out.reshape(chan_count, own, in_local * B0), "chan", 0, 0, tiled=True)
    input_grad = out.reshape(group, -1).astype(F32)

    def split_columns(rows):
        return jnp.transpose(rows.reshape(rows.shape[0], chan_count, columns), (1, 0, 2))

    g = grad_one.reshape(3, 2, in_channels, 2, wide)
    g = jnp.stack([g[:, 1, :, 1], g[:, 0, :, 0], g[:, 1, :, 0]], axis=1).reshape(9, in_channels, wide)
    g = jnp.concatenate([jnp.transpose(g, (1, 0, 2)).reshape(-1, wide), grad_short], axis=0)
    parts = split_columns(g).reshape(chan_count, frame_count, -1, columns)
    layers = []
    for grad in (grad_two, grad_three, grad_four):
        rows = jnp.transpose(grad.reshape(3, wide, 3, wide), (1, 0, 2, 3)).reshape(-1, wide)
        layers.append(split_columns(rows).reshape(chan_count, frame_count, -1, columns))
    parts = jnp.concatenate([parts] + layers, axis=2)
    mine = scatter_sum(parts, "chan")[0]
    mine = scatter_sum(mine, "frames")[0].astype(F32)
    grad_first = mine[: first_weight.shape[0]]
    grad_wide = mine[first_weight.shape[0] :].reshape(wide_weight.shape)

    norm_sums = [norm_zero, norm_one, norm_two, norm_three]
    grad_norms = jnp.stack([pack_norms([s[1] for s in norm_sums]), pack_norms([s[0] for s in norm_sums])])
    grad_norms = lax.dynamic_slice_in_dim(grad_norms, chan * norm_params.shape[2], norm_params.shape[2], 2)
    own_squares = jnp.sum(grad_first * grad_first) + jnp.sum(grad_wide * grad_wide)
    own_squares = own_squares + jnp.where(lax.axis_index("frames") == 0, jnp.sum(grad_norms * grad_norms), 0.0)
    squares = total_sum(jnp.broadcast_to(own_squares, (1, 128)))[0, 0]
    grad_norm = jnp.sqrt(squares)
    factor = clip_limit / jnp.maximum(grad_norm, clip_limit)
    first_next, first_mean_next, first_square_next = adam_step(
        first_weight, first_mean, first_square, grad_first * factor, conv_rate, weight_decay
    )
    wide_next, wide_mean_next, wide_square_next = adam_step(
        wide_weight, wide_mean, wide_square, grad_wide * factor, conv_rate, weight_decay
    )
    norm_next, norm_mean_next, norm_square_next = adam_step(
        norm_params, norm_mean, norm_square, grad_norms * factor, norm_rate, 0.0
    )
    return (
        block_out,
        input_grad,
        grad_norm,
        first_next,
        first_mean_next,
        first_square_next,
        first_next.astype(BF16),
        wide_next,
        wide_mean_next,
        wide_square_next,
        wide_next.astype(BF16),
        norm_next,
        norm_mean_next,
        norm_square_next,
    )


def solution(mesh):
    rows = P("frames", "chan")
    deep = P(None, "frames", "chan")
    norms = P(None, None, "chan")
    in_specs = (rows, P("frames"), rows, rows, rows, rows, deep, deep, deep, norms, norms, norms)
    out_specs = (rows, rows, P(), rows, rows, rows, rows, deep, deep, deep, deep, norms, norms, norms)
    return jax.shard_map(body, mesh=mesh, in_specs=in_specs, out_specs=out_specs, check_vma=False)
```

time: 1660 us -> 655 us (0.39)
  matrix products: 556 us -> 0 us
  local copies, waits for them, and re-layouts: 543 us -> 210 us
  blocking collectives: 275 us -> 51.6 us
  Pallas kernels: 0 us -> 129 us
  other arithmetic: 114 us -> 50.9 us
  starting transfers between devices: 42.2 us -> 79.7 us
  waiting for transfers between devices: 88.4 us -> 107 us
    dot_general x111 -> x0, matrix products: 556 us -> none  [the longest x36 250 us: conv_grad_input(): jnp.einsum('fbo,io->fbi', rows_used, taps[:, 3 * time_tap + freq_tap], pr...]
    slice x26 -> x17, local copies, waits for them, and re-layouts: 277 us -> 37.4 us  [the longest x4 30.5 us: body(): taps = [wide_all[k].reshape(3, 3 * wide, wide) for k in range(3)]]
    psum x9 -> x0, blocking collectives: 199 us -> none  [the longest x4 86 us: statistics(): lax.psum((jnp.sum(values, axis=(0, 1)), jnp.sum(values * values, axis=(0,...]
    pallas_call x0 -> x8, Pallas kernels: none -> 129 us  [run(): pl.pallas_call(kernel, in_specs=[SMEM] * len(masks) + [VMEM] * len(operan...]
    all_to_all x0 -> x13, starting transfers between devices: none -> 56.9 us  [the longest x9 40.6 us: total_sum(): return jnp.sum(lax.all_to_all(copies, BOTH, 0, 0, tiled=True), axis=0)]
    unnamed x381 -> x88, local copies, waits for them, and re-layouts: 61.5 us -> 6.28 us
    reshape x9 -> x14, local copies, waits for them, and re-layouts: 8.34 us -> 60.6 us  [the longest x1 19.1 us: body(): wide_all = wide_all.reshape(frame_count, chan_count, 3, -1, 9, columns)]
    all_to_all x0 -> x13, waiting for transfers between devices: none -> 50.6 us  [the longest x9 38.8 us: total_sum(): return jnp.sum(lax.all_to_all(copies, BOTH, 0, 0, tiled=True), axis=0)]
  transfers between devices with their start and end apart: 28 -> 25, of which waited for: 6 -> 9; matrix products, arithmetic and copies ran while one was open for 45% -> 33% of each run, Pallas kernels for 0% -> 4%
where the time goes in v1:
time: 655 us; the launch traced here: 646 us
  local copies, waits for them, and re-layouts  210 us (32%)
  Pallas kernels  129 us (20%)
  waiting for transfers between devices  107 us (16%)
  starting transfers between devices  79.7 us (12%)
  blocking collectives  51.6 us (8%)
  other arithmetic  50.9 us (8%)
  between operations  18.6 us (3%)
    pallas_call x8, Pallas kernels, run(): pl.pallas_call(kernel, in_specs=[SMEM] * len(masks) + [VMEM] * len(operan...  129 us
    ppermute x5, waiting for transfers between devices, scatter_sum(): came = lax.ppermute(send, axis, [(i, i ^ step) for i in range(size)])  56 us
    all_gather x1, blocking collectives, body(): lax.all_gather(first_weight.astype(BF16), ('frames', 'chan'), axis=0)  46.1 us
    all_to_all x9, starting transfers between devices, total_sum(): return jnp.sum(lax.all_to_all(copies, BOTH, 0, 0, tiled=True), axis=0)  40.6 us
    all_to_all x9, waiting for transfers between devices, total_sum(): return jnp.sum(lax.all_to_all(copies, BOTH, 0, 0, tiled=True), axis=0)  38.8 us
    slice x4, local copies, waits for them, and re-layouts, body(): taps = [wide_all[k].reshape(3, 3 * wide, wide) for k in range(3)]  30.5 us
    reshape x1, local copies, waits for them, and re-layouts, body(): wide_all = wide_all.reshape(frame_count, chan_count, 3, -1, 9, columns)  19.1 us
    another operation x3, local copies, waits for them, and re-layouts, split_columns(): rows.reshape(rows.shape[0], chan_count, columns)  14.2 us
  transfers between devices with their start and end apart: 25, of which 9 were waited for; matrix products, arithmetic and copies ran while one was open for 33% of the time, Pallas kernels for 4%

profile of v1, /device:TPU:0, one launch (start us, length us, event | category | flops | bytes accessed | tf_op | source)
XLA Modules:
  0.0 646.3 jit_solution(15665007567478410298)
XLA Ops:
  10.3 5.4 collective-permute-start
  19.9 7.1 %all-to-all-start.1 = ((f32[32,2,128]{2,1,0:T(2,128)}), f32[32,2,128]{2,1,0:T(2,128)S(1)}, u32[]{:S(2)}, u32[]{:S(2)}) async-start(f32[32,2,128]{2,1,0:T(2,128)} %broadcast_in_dim.19), calls=%async_computation.1 | async-start | bytes 65536 | tf_op jit(solution)/shard_map/all_to_all | solution.py:34
  36.9 46.1 %all-gather.2 = bf16[32,160,64]{1,2,0:T(8,128)(2,1)S(1)} all-gather(bf16[1,160,64]{1,2,0:T(8,128)(2,1)S(1)} %convert_bitcast_fusion), channel_id=2, replica_groups=mesh['chan'=4,'frames'=8] {'frames','chan'}, dimensions={0}, use_global_device_ids=true | all-gather | bytes 675840 | tf_op jit(solution)/shard_map/all_gather | solution.py:456
  84.8 5.4 all_gather.15
  110.3 11.8 %all-to-all-done = bf16[4,96,2048]{2,1,0:T(8,128)(2,1)} async-done(((bf16[4,96,2048]{2,1,0:T(8,128)(2,1)}), bf16[4,96,2048]{2,1,0:T(8,128)(2,1)}, u32[]{:S(2)}, u32[]{:S(2)}) %all-to-all-start) | async-done | bytes 1572896 | tf_op jit(solution)/shard_map/all_to_all | solution.py:51
  128.4 9.5 %shard_map.227 = (f32[96,32,256]{2,1,0:T(8,128)}, f32[96,32,256]{2,1,0:T(8,128)}, bf16[2,96,32,128]{3,2,1,0:T(8,128)(2,1)}, f32[2,8,256]{2,1,0:T(8,128)}) custom-call(f32[96]{0:T(128)} %get-tuple-element.233.prev_ref, f32[96]{0:T(128)} %get-tuple-element.232.next_ref, bf16[2,96,32,128]{3,2,1,0:T(8,128)(2,1)} %copy.505.x_ref, ...), custom_call_target="tpu_custom_call" | custom-call | tf_op jit(solution)/shard_map/pallas_call | solution.py:373
  143.7 5.9 all-to-all-done.2
  154.7 14.0 %copy.508 = bf16[96,288,64]{2,0,1:T(8,128)(2,1)} copy(bf16[96,288,64]{1,2,0:T(8,128)(2,1)} %all-gather.5.cloned.1.call-done) | data formatting | bytes 7077888 | tf_op jit(solution)/shard_map/all_gather | solution.py:459
  168.7 19.1 %reshape.182 = bf16[8,4,3,32,9,64]{5,2,1,0,4,3:T(4,128)(2,1)} reshape(bf16[96,288,64]{2,0,1:T(8,128)(2,1)} %copy.508) | data formatting | bytes 7077888 | tf_op jit(solution)/shard_map/reshape | solution.py:460
  187.7 20.6 %fusion.25 = (bf16[1,9,8,32,4,64]{5,0,4,2,1,3:T(2,128)(2,1)}, bf16[1,9,8,32,4,64]{5,0,4,2,1,3:T(2,128)(2,1)}, bf16[1,9,8,32,4,64]{5,0,4,2,1,3:T(2,128)(2,1)S(1)}) fusion(bf16[3,9,8,32,4,64]{5,0,4,2,1,3:T(4,128)(2,1)} %bitcast.147), kind=kLoop, calls=%fused_computation.119 | loop fusion | bytes 7077888 | tf_op jit(solution)/shard_map/slice | solution.py:465
  212.1 11.7 %shard_map.228 = (f32[96,32,256]{2,1,0:T(8,128)}, bf16[96,32,256]{2,1,0:T(8,128)(2,1)}, f32[2,8,256]{2,1,0:T(8,128)}) custom-call(f32[96]{0:T(128)} %get-tuple-element.233.prev_ref, f32[96]{0:T(128)} %get-tuple-element.232.next_ref, f32[96,32,256]{2,1,0:T(8,128)} %get-tuple-element.39.h_ref.low_ref, f32[4,256]{1,0:T(4,128)} %pad_maximum_fusion.9.vec_ref.low_vec_ref, ...), custom_call_target="tpu_custom_call" | custom-call | tf_op jit(solution)/shard_map/pallas_call | solution.py:373
  236.0 10.5 %copy.516 = bf16[3,9,8,32,4,64]{5,4,3,2,1,0:T(4,128)(2,1)} copy(bf16[3,9,8,32,4,64]{5,0,4,2,1,3:T(4,128)(2,1)} %bitcast.148) | data formatting | bytes 7077888 | tf_op jit(solution)/shard_map/transpose | solution.py:461
  246.5 9.7 %reshape.185 = bf16[3,9,256,256]{3,2,1,0:T(8,128)(2,1)S(1)} reshape(bf16[3,9,8,32,4,64]{5,4,3,2,1,0:T(4,128)(2,1)} %copy.516) | data formatting | bytes 7077888 | tf_op jit(solution)/shard_map/reshape | solution.py:461
  267.9 10.9 %shard_map.229 = (f32[96,32,256]{2,1,0:T(8,128)}, bf16[96,32,256]{2,1,0:T(8,128)(2,1)}, f32[2,8,256]{2,1,0:T(8,128)}) custom-call(f32[96]{0:T(128)} %get-tuple-element.233.prev_ref, f32[96]{0:T(128)} %get-tuple-element.232.next_ref, f32[96,32,256]{2,1,0:T(8,128)} %get-tuple-element.42.h_ref.x_ref.low_ref, f32[4,256]{1,0:T(4,128)} %pad_maximum_fusion.10.vec_ref.low_vec_ref, ...), custom_call_target="tpu_custom_call" | custom-call | tf_op jit(solution)/shard_map/pallas_call | solution.py:373
  280.1 6.1 all-to-all-start.5
  298.5 27.0 %shard_map.230 = (bf16[84,32,256]{2,1,0:T(8,128)(2,1)}, f32[96,32,256]{2,1,0:T(8,128)}, f32[2,8,256]{2,1,0:T(8,128)}, bf16[3,256,768]{2,1,0:T(8,128)(2,1)}) custom-call(f32[96]{0:T(128)} %get-tuple-element.233.prev_ref, f32[96]{0:T(128)} %get-tuple-element.232.next_ref, f32[96,32,256]{2,1,0:T(8,128)} %get-tuple-element.44.h_ref, ...), custom_call_target="tpu_custom_call" | custom-call | tf_op jit(solution)/shard_map/pallas_call | solution.py:373
  327.0 5.9 all-to-all-start.7
  340.9 22.2 %shard_map.231 = (f32[96,32,256]{2,1,0:T(8,128)}, f32[2,8,256]{2,1,0:T(8,128)}, bf16[3,256,768]{2,1,0:T(8,128)(2,1)}) custom-call(f32[96]{0:T(128)} %get-tuple-element.233.prev_ref, f32[96]{0:T(128)} %get-tuple-element.232.next_ref, f32[96,32,256]{2,1,0:T(8,128)} %get-tuple-element.47.dz_ref, f32[96,32,256]{2,1,0:T(8,128)} %get-tuple-element.44.h_ref, ...), custom_call_target="tpu_custom_call" | custom-call | tf_op jit(solution)/shard_map/pallas_call | solution.py:373
  375.2 24.9 %shard_map.232 = (f32[96,32,256]{2,1,0:T(8,128)}, f32[2,8,256]{2,1,0:T(8,128)}, bf16[3,256,768]{2,1,0:T(8,128)(2,1)}, bf16[128,256]{1,0:T(8,128)(2,1)}, bf16[96,32,256]{2,1,0:T(8,128)(2,1)}) custom-call(f32[96]{0:T(128)} %get-tuple-element.233.prev_ref, f32[96]{0:T(128)} %get-tuple-element.232.next_ref, f32[96,32,256]{2,1,0:T(8,128)} %get-tuple-element.50.dz_ref, ...), custom_call_target="tpu_custom_call" | custom-call | tf_op jit(solution)/shard_map/pallas_call | solution.py:373
  443.2 18.5 %shard_map.233 = (f32[2,84,32,128]{3,2,1,0:T(8,128)}, f32[2,8,128]{2,1,0:T(8,128)}, bf16[3,256,512]{2,1,0:T(8,128)(2,1)}) custom-call(f32[96]{0:T(128)} %get-tuple-element.233.prev_ref, f32[96]{0:T(128)} %get-tuple-element.232.next_ref, f32[96,32,256]{2,1,0:T(8,128)} %get-tuple-element.54.dz_ref, f32[96,32,256]{2,1,0:T(8,128)} %get-tuple-element.39.h_ref.low_ref, ...), custom_call_target="tpu_custom_call" | custom-call | tf_op jit(solution)/shard_map/pallas_call | solution.py:373
  466.1 6.0 pad_maximum_fusion.3
  484.1 46.1 %collective-permute-done.6 = bf16[2,8,1024,64]{2,1,3,0:T(8,128)(2,1)} collective-permute-done((bf16[2,8,1024,64]{2,1,3,0:T(8,128)(2,1)S(1)}, bf16[2,8,1024,64]{2,1,3,0:T(8,128)(2,1)}, u32[]{:S(2)}, u32[]{:S(2)}) %collective-permute-start.6) | collective-permute-done | bytes 2097184 | tf_op jit(solution)/shard_map/ppermute | solution.py:70
  555.3 19.5 %all-to-all-done.10 = f32[32,2,128]{2,1,0:T(2,128)S(1)} async-done(((f32[32,2,128]{2,1,0:T(2,128)}), f32[32,2,128]{2,1,0:T(2,128)S(1)}, u32[]{:S(2)}, u32[]{:S(2)}) %all-to-all-start.10) | async-done | bytes 32800 | tf_op jit(solution)/shard_map/all_to_all | solution.py:34
  611.0 5.4 collective-permute-done.10
  (295 shorter events, 258.3 us)
Async XLA Ops:
  7.2 147.5 %all-gather.5.cloned.1.call-start = ((), (), s32[]{:S(2)}) async-start(), calls=%async_computation.13 | async-start | bytes 4866048 | tf_op jit(solution)/shard_map/all_gather | solution.py:459
  10.3 96.7 %collective-permute-start = (s32[7]{0:T(128)}, s32[7]{0:T(128)}, u32[]{:S(2)}, u32[]{:S(2)}) collective-permute-start(s32[7]{0:T(128)} %get-tuple-element.226), channel_id=1, source_target_pairs={{0,1},{1,2},{2,3},{3,4},{4,5},{5,6},{6,7},{8,9},{9,10},{10,11},{11... | collective-permute-start | bytes 92 | tf_op jit(solution)/shard_map/ppermute | solution.py:41
  15.7 91.3 %collective-permute-start.1 = (s32[7]{0:T(128)}, s32[7]{0:T(128)}, u32[]{:S(2)}, u32[]{:S(2)}) collective-permute-start(s32[7]{0:T(128)} %get-tuple-element.227), channel_id=1, source_target_pairs={{1,0},{2,1},{3,2},{4,3},{5,4},{6,5},{7,6},{9,8},{10,9},{11,10},{12... | collective-permute-start | bytes 92 | tf_op jit(solution)/shard_map/ppermute | solution.py:42
  19.9 77.5 %all-to-all-start.1 = ((f32[32,2,128]{2,1,0:T(2,128)}), f32[32,2,128]{2,1,0:T(2,128)S(1)}, u32[]{:S(2)}, u32[]{:S(2)}) async-start(f32[32,2,128]{2,1,0:T(2,128)} %broadcast_in_dim.19), calls=%async_computation.1 | async-start | bytes 65536 | tf_op jit(solution)/shard_map/all_to_all | solution.py:34
  27.8 80.6 %collective-permute-start.4 = (bf16[6,2048]{1,0:T(8,128)(2,1)S(1)}, bf16[6,2048]{1,0:T(8,128)(2,1)S(1)}, u32[]{:S(2)}, u32[]{:S(2)}) collective-permute-start(bf16[6,2048]{1,0:T(8,128)(2,1)S(1)} %get-tuple-element.201), channel_id=1, source_target_pairs={{0,1},{1,2},{2,3},{3,4},{4,5},{5,6},{6,7},{8,9},{9,10},{10,11},{11... | collective-permute-start | bytes 73736 | tf_op jit(solution)/shard_map/ppermute | solution.py:41
  31.5 62.1 %collective-permute-start.2 = (bf16[6,2048]{1,0:T(8,128)(2,1)S(1)}, bf16[6,2048]{1,0:T(8,128)(2,1)}, u32[]{:S(2)}, u32[]{:S(2)}) collective-permute-start(bf16[6,2048]{1,0:T(8,128)(2,1)S(1)} %get-tuple-element.207), channel_id=1, source_target_pairs={{0,1},{1,2},{2,3},{3,4},{4,5},{5,6},{6,7},{8,9},{9,10},{10,11},{11... | collective-permute-start | bytes 73736 | tf_op jit(solution)/shard_map/ppermute | solution.py:41
  35.5 59.4 %collective-permute-start.3 = (bf16[6,2048]{1,0:T(8,128)(2,1)S(1)}, bf16[6,2048]{1,0:T(8,128)(2,1)}, u32[]{:S(2)}, u32[]{:S(2)}) collective-permute-start(bf16[6,2048]{1,0:T(8,128)(2,1)S(1)} %get-tuple-element.208), channel_id=1, source_target_pairs={{1,0},{2,1},{3,2},{4,3},{5,4},{6,5},{7,6},{9,8},{10,9},{11,10},{12... | collective-permute-start | bytes 73736 | tf_op jit(solution)/shard_map/ppermute | solution.py:42
  93.6 14.8 %collective-permute-start.5 = (bf16[6,2048]{1,0:T(8,128)(2,1)S(1)}, bf16[6,2048]{1,0:T(8,128)(2,1)S(1)}, u32[]{:S(2)}, u32[]{:S(2)}) collective-permute-start(bf16[6,2048]{1,0:T(8,128)(2,1)S(1)} %get-tuple-element.202), channel_id=1, source_target_pairs={{1,0},{2,1},{3,2},{4,3},{5,4},{6,5},{7,6},{9,8},{10,9},{11,10},{12... | collective-permute-start | bytes 73736 | tf_op jit(solution)/shard_map/ppermute | solution.py:42
  97.4 24.7 %all-to-all-start = ((bf16[4,96,2048]{2,1,0:T(8,128)(2,1)}), bf16[4,96,2048]{2,1,0:T(8,128)(2,1)}, u32[]{:S(2)}, u32[]{:S(2)}) async-start(bf16[4,96,2048]{2,1,0:T(8,128)(2,1)} %pad_maximum_fusion.1), calls=%async_computation | async-start | bytes 3145728 | tf_op jit(solution)/shard_map/all_to_all | solution.py:51
  139.3 10.3 %all-to-all-start.2 = ((f32[32,2,256]{2,1,0:T(2,128)}), f32[32,2,256]{2,1,0:T(2,128)S(1)}, u32[]{:S(2)}, u32[]{:S(2)}) async-start(f32[32,2,256]{2,1,0:T(2,128)} %broadcast_in_dim.20), calls=%async_computation.2 | async-start | bytes 131072 | tf_op jit(solution)/shard_map/all_to_all | solution.py:34
  149.6 75.0 %all-to-all-start.4 = ((bf16[4,96,2048]{2,1,0:T(8,128)(2,1)}), bf16[4,96,2048]{2,1,0:T(8,128)(2,1)}, u32[]{:S(2)}, u32[]{:S(2)}) async-start(bf16[4,96,2048]{2,1,0:T(8,128)(2,1)} %pad_maximum_fusion.2), calls=%async_computation.4 | async-start | bytes 3145728 | tf_op jit(solution)/shard_map/all_to_all | solution.py:51
  225.3 40.4 %all-to-all-start.3 = ((f32[32,2,256]{2,1,0:T(2,128)}), f32[32,2,256]{2,1,0:T(2,128)}, u32[]{:S(2)}, u32[]{:S(2)}) async-start(f32[32,2,256]{2,1,0:T(2,128)} %broadcast_in_dim.21), calls=%async_computation.3 | async-start | bytes 131072 | tf_op jit(solution)/shard_map/all_to_all | solution.py:34
  280.1 16.9 %all-to-all-start.5 = ((f32[32,2,256]{2,1,0:T(2,128)}), f32[32,2,256]{2,1,0:T(2,128)}, u32[]{:S(2)}, u32[]{:S(2)}) async-start(f32[32,2,256]{2,1,0:T(2,128)} %broadcast_in_dim.22), calls=%async_computation.5 | async-start | bytes 131072 | tf_op jit(solution)/shard_map/all_to_all | solution.py:34
  327.0 13.2 %all-to-all-start.7 = ((f32[32,2,256]{2,1,0:T(2,128)}), f32[32,2,256]{2,1,0:T(2,128)S(1)}, u32[]{:S(2)}, u32[]{:S(2)}) async-start(f32[32,2,256]{2,1,0:T(2,128)} %broadcast_in_dim.23), calls=%async_computation.7 | async-start | bytes 131072 | tf_op jit(solution)/shard_map/all_to_all | solution.py:34
  364.5 10.1 %all-to-all-start.8 = ((f32[32,2,256]{2,1,0:T(2,128)}), f32[32,2,256]{2,1,0:T(2,128)S(1)}, u32[]{:S(2)}, u32[]{:S(2)}) async-start(f32[32,2,256]{2,1,0:T(2,128)} %broadcast_in_dim.24), calls=%async_computation.8 | async-start | bytes 131072 | tf_op jit(solution)/shard_map/all_to_all | solution.py:34
  401.6 40.1 %all-to-all-start.9 = ((f32[32,2,256]{2,1,0:T(2,128)}), f32[32,2,256]{2,1,0:T(2,128)}, u32[]{:S(2)}, u32[]{:S(2)}) async-start(f32[32,2,256]{2,1,0:T(2,128)} %broadcast_in_dim.25), calls=%async_computation.9 | async-start | bytes 131072 | tf_op jit(solution)/shard_map/all_to_all | solution.py:34
  482.4 47.9 %collective-permute-start.6 = (bf16[2,8,1024,64]{2,1,3,0:T(8,128)(2,1)S(1)}, bf16[2,8,1024,64]{2,1,3,0:T(8,128)(2,1)}, u32[]{:S(2)}, u32[]{:S(2)}) collective-permute-start(bf16[2,8,1024,64]{2,1,3,0:T(8,128)(2,1)S(1)} %constant_dynamic-slice_fusion.3), channel_id=1, source_target_pairs={{0,16},{8,24},{16,0},{24,8},{1,17},{9,25},{17,1},{25,9},{2,18},{10... | collective-permute-start | bytes 6291464 | tf_op jit(solution)/shard_map/ppermute | solution.py:70
  546.2 49.3 %collective-permute-start.8 = (bf16[4,1024,64]{1,0,2:T(4,128)(2,1)}, bf16[4,1024,64]{1,0,2:T(4,128)(2,1)}, u32[]{:S(2)}, u32[]{:S(2)}) collective-permute-start(bf16[4,1024,64]{1,0,2:T(4,128)(2,1)} %dynamic-slice_bitcast_fusion), channel_id=1, source_target_pairs={{0,4},{1,5},{2,6},{3,7},{4,0},{5,1},{6,2},{7,3},{8,12},{9,13},{10,... | collective-permute-start | bytes 1572872 | tf_op jit(solution)/shard_map/ppermute | solution.py:70
  550.6 24.3 %all-to-all-start.10 = ((f32[32,2,128]{2,1,0:T(2,128)}), f32[32,2,128]{2,1,0:T(2,128)S(1)}, u32[]{:S(2)}, u32[]{:S(2)}) async-start(f32[32,2,128]{2,1,0:T(2,128)} %broadcast_in_dim.26), calls=%async_computation.10 | async-start | bytes 65536 | tf_op jit(solution)/shard_map/all_to_all | solution.py:34
  574.9 23.7 %all-to-all-start.6 = ((bf16[4,84,2048]{2,1,0:T(8,128)(2,1)}), bf16[4,84,2048]{2,1,0:T(8,128)(2,1)S(1)}, u32[]{:S(2)}, u32[]{:S(2)}) async-start(bf16[4,84,2048]{2,1,0:T(8,128)(2,1)} %copy.521), calls=%async_computation.6 | async-start | bytes 2883584 | tf_op jit(solution)/shard_map/all_to_all | solution.py:556
  597.7 8.9 %collective-permute-start.9 = (bf16[2,1024,64]{1,0,2:T(2,128)(2,1)S(1)}, bf16[2,1024,64]{1,0,2:T(2,128)(2,1)}, u32[]{:S(2)}, u32[]{:S(2)}) collective-permute-start(bf16[2,1024,64]{1,0,2:T(2,128)(2,1)S(1)} %constant_dynamic-slice_fusion.1), channel_id=1, source_target_pairs={{0,2},{1,3},{2,0},{3,1},{4,6},{5,7},{6,4},{7,5},{8,10},{9,11},{10,... | collective-permute-start | bytes 786440 | tf_op jit(solution)/shard_map/ppermute | solution.py:70
  598.5 22.5 %all-to-all-start.11 = ((bf16[4,84,2048]{2,1,0:T(8,128)(2,1)}), bf16[4,84,2048]{2,1,0:T(8,128)(2,1)S(1)}, u32[]{:S(2)}, u32[]{:S(2)}) async-start(bf16[4,84,2048]{2,1,0:T(8,128)(2,1)} %copy.537), calls=%async_computation.11 | async-start | bytes 2883584 | tf_op jit(solution)/shard_map/all_to_all | solution.py:559
  608.4 8.1 %collective-permute-start.10 = (bf16[1,1024,64]{1,0,2:T(2,128)(2,1)S(1)}, bf16[1,1024,64]{1,0,2:T(2,128)(2,1)}, u32[]{:S(2)}, u32[]{:S(2)}) collective-permute-start(bf16[1,1024,64]{1,0,2:T(2,128)(2,1)S(1)} %constant_dynamic-slice_fusion), channel_id=1, source_target_pairs={{0,1},{1,0},{2,3},{3,2},{4,5},{5,4},{6,7},{7,6},{8,9},{9,8},{10,11... | collective-permute-start | bytes 393224 | tf_op jit(solution)/shard_map/ppermute | solution.py:70
  621.6 11.7 %all-to-all-start.12 = ((f32[32,1,128]{2,1,0:T(1,128)}), f32[32,1,128]{2,1,0:T(1,128)S(1)}, u32[]{:S(2)}, u32[]{:S(2)}) async-start(f32[32,1,128]{2,1,0:T(1,128)} %broadcast_in_dim_broadcast_in_dim_broadcast_in_dim.3), calls=%async_computation.12 | async-start | bytes 32768 | tf_op jit(solution)/shard_map/all_to_all | solution.py:34
  (41 other events, 416.1 us)
Sparse Core Ops, SparseCore 0:
  11.5 70.4 all-gather.4

commit v2 on v0

v2 whole, which is shorter than its diff:
```python
import functools
import math

import jax
import jax.numpy as jnp
from jax import lax
from jax.experimental import pallas as pl
from jax.experimental.pallas import tpu as pltpu
from jax.sharding import PartitionSpec as P

B0 = 64
STEP = 10
B1 = 32
HALO = 6
LANES = 128

norm_epsilon = 1e-05
clip_limit = 100.0
beta_first = 0.9
beta_second = 0.999
adam_epsilon = 1e-08
conv_rate = 0.05
norm_rate = 0.5
weight_decay = 0.01

BOTH = ("chan", "frames")
VMEM_BYTES = 58 * 1024 * 1024
F32 = jnp.float32
BF16 = jnp.bfloat16
NT = (((1,), (1,)), ((), ()))


def to_all(copies):
    return lax.all_to_all(copies, BOTH, 0, 0, tiled=True)


def to_frames(block):
    parts = lax.axis_size("chan")
    count = lax.axis_size("frames")
    chan = lax.axis_index("chan")
    own = block.shape[0] // parts
    forward = [(i, i + 1) for i in range(count - 1)]
    backward = [(b, a) for a, b in forward]
    padded = jnp.pad(block, ((HALO, HALO), (0, 0), (0, 0)))
    windows = [lax.dynamic_slice_in_dim(padded, (chan ^ d) * own, own + 2 * HALO, 0) for d in range(parts)]
    swaps = [[(i, i ^ d) for i in range(parts)] for d in range(parts)]
    came = list(windows)
    for d in range(parts - 1, 0, -1):
        came[d] = lax.ppermute(windows[d], "chan", swaps[d])
    low = lax.ppermute(block[block.shape[0] - HALO :], "frames", forward)
    high = lax.ppermute(block[:HALO], "frames", backward)
    edge = jnp.concatenate([low, high], axis=0)
    edges = [edge] + [lax.ppermute(edge, "chan", swaps[d]) for d in range(1, parts)]
    return came, edges, windows


def halves(axis, size):
    steps = []
    while size > 1:
        size //= 2
        steps.append((axis, size))
    return steps


def code_of(order, place):
    return sum(((place[axis] // step) % 2) << k for k, (axis, step) in enumerate(order))


def scatter_steps(keeps, sends, order):
    steps = order[::-1]
    for number, (axis, step) in enumerate(steps):
        size = lax.axis_size(axis)
        swap = [(i, i ^ step) for i in range(size)]
        came = [lax.ppermute(send, axis, swap) for send in sends]
        half = keeps[0].shape[0] // 2

        def added(part):
            return jnp.concatenate([(k[part].astype(F32) + c[part].astype(F32)).astype(BF16) for k, c in zip(keeps, came)], axis=1)

        if number + 1 == len(steps):
            return added(slice(None))[0]
        keeps, sends = [added(slice(0, half))], [added(slice(half, None))]


def after(value, *others):
    return lax.optimization_barrier((value, *others))[0]


def fit(count, target, unit=1):
    return max([k for k in range(unit, target + 1, unit) if count % k == 0], default=count)


def loop(low, high, target, body, unit=1):
    return spans(low, high - low, target, body, unit)


def spans(low, count, target, body, unit=1):
    chunk = fit(count, target, unit)

    def step(i, carry):
        body(low + i * chunk, chunk, i)
        return carry

    if chunk == count:
        body(low, chunk, 0)
    else:
        lax.fori_loop(0, count // chunk, step, 0)
    return chunk


class Fetched:
    def __init__(self, source, ref, sems):
        self.source, self.ref, self.sems = source, ref, sems
        self.pieces = sems.shape[0]
        self.size = ref.shape[0] // self.pieces

    def copy(self, number):
        rows = pl.ds(number * self.size, self.size)
        return pltpu.make_async_copy(self.source.at[rows], self.ref.at[rows], self.sems.at[number])

    def start(self):
        for number in range(self.pieces):
            self.copy(number).start()

    def need(self, number):
        self.copy(number).wait()

    def need_all(self):
        for number in range(self.pieces):
            self.need(number)


class Sent:
    def __init__(self, target, ref, sems):
        self.target, self.ref, self.sems = target, ref, sems
        self.shape, self.dtype = ref.shape, ref.dtype

    def copy(self, base, chunk, number):
        rows = pl.ds(base, chunk)
        return pltpu.make_async_copy(self.ref.at[rows], self.target.at[rows], self.sems.at[number])

    def send(self, base, chunk, number):
        self.copy(base, chunk, number).start()

    def finish(self, low, high, chunk):
        for number in range((high - low) // chunk):
            self.copy(low + number * chunk, chunk, number).wait()


def sigmoid(z):
    return 0.5 * jnp.tanh(0.5 * z) + 0.5


def dot(a, b):
    return jnp.dot(a, b, preferred_element_type=F32)


def dot_nt(a, b):
    return lax.dot_general(a, b, NT, preferred_element_type=F32)


def chosen(rows, columns, source):
    r = lax.broadcasted_iota(jnp.int32, (rows, columns), 0)
    c = lax.broadcasted_iota(jnp.int32, (rows, columns), 1)
    return (c == source(r)).astype(BF16)


def same(r):
    return r


def transposed(rows):
    return dot_nt(chosen(rows.shape[1], rows.shape[1], same), rows).astype(BF16)


def shifts(flat):
    rows = flat.shape[0]
    bins = lax.broadcasted_iota(jnp.int32, flat.shape, 0) % B1
    below = jnp.where(bins == 0, 0.0, pltpu.roll(flat, 1, 0))
    above = jnp.where(bins == B1 - 1, 0.0, pltpu.roll(flat, rows - 1, 0))
    return below, above


def mask_frames(partial, mask_ref, base, chunk):
    cube = partial.reshape(chunk, B1, partial.shape[-1])
    return jnp.concatenate([cube[k] * mask_ref[base + k] for k in range(chunk)], axis=0)


def rows_of(ref, base, chunk):
    return ref[pl.ds(base, chunk)].reshape(chunk * B1, ref.shape[-1])


def put(ref, base, chunk, value):
    ref[pl.ds(base, chunk)] = value.reshape(chunk, B1, value.shape[-1]).astype(ref.dtype)


def taps_sum(cols_ref, taps_ref, masks, base, chunk, product=dot):
    total = None
    for tap in (1, 0, 2):
        partial = product(rows_of(cols_ref, base + tap - 1, chunk), taps_ref[tap])
        if tap == 0:
            partial = mask_frames(partial, masks[0], base, chunk)
        if tap == 2:
            partial = mask_frames(partial, masks[1], base, chunk)
        total = partial if total is None else total + partial
    return total


def own_rows(value, base, chunk, low, high):
    frame = base + lax.broadcasted_iota(jnp.int32, value.shape, 0) // B1
    return jnp.where((frame >= low) & (frame < high), value, 0.0)


def add_sums(acc_ref, first, second):
    rows, channels = first.shape
    acc_ref[0] += jnp.sum(first.reshape(rows // 8, 8, channels), axis=0)
    acc_ref[1] += jnp.sum(second.reshape(rows // 8, 8, channels), axis=0)


def spread_sums(acc_ref, copies_ref):
    channels = acc_ref.shape[-1]
    for k in range(2):
        row = jnp.sum(acc_ref[k], axis=0, keepdims=True)
        copies_ref[:, :, k * channels : (k + 1) * channels] = jnp.broadcast_to(
            row[None], (copies_ref.shape[0], 1, channels)
        )


def came_sums(came_ref):
    total = jnp.sum(came_ref[...], axis=0)
    half = total.shape[-1] // 2
    return total[:, :half], total[:, half:]


def norm_of(came_ref, pair_ref, count):
    first, second = came_sums(came_ref)
    mean = first / count
    spread = lax.rsqrt(second / count - mean * mean + norm_epsilon)
    return mean, spread, pair_ref[0:1], pair_ref[1:2]


def norm_rows(vec_ref):
    return vec_ref[0:1], vec_ref[1:2], vec_ref[2:3], vec_ref[3:4]


def normal(values, norm):
    return (values.astype(F32) - norm[0]) * norm[1]


def activated(values, norm):
    z = normal(values, norm) * norm[2] + norm[3]
    return z * sigmoid(z)


def back_act(q, values, norm):
    xhat = normal(values, norm)
    z = xhat * norm[2] + norm[3]
    gate = sigmoid(z)
    return q * gate * (1.0 + z * (1.0 - gate)), xhat


def back_norm(dz, values, norm, sums, count):
    xhat = normal(values, norm)
    return norm[2] * norm[1] * (dz.astype(F32) - sums[0] / count - xhat * (sums[1] / count))


def swap_halves(value):
    return pltpu.roll(value, LANES // 2, 1)


def halves_of(first, second):
    low = lax.broadcasted_iota(jnp.int32, first.shape, 1) < LANES // 2
    return jnp.where(low, first, swap_halves(second)), jnp.where(low, swap_halves(first), second)


def unpack_wide(layer, chans, all_ref, taps_out, came_ref, sems):
    fetch = pltpu.make_async_copy(all_ref.at[:, layer], came_ref, sems.at[0])
    fetch.start()
    devices, groups, rows, _ = came_ref.shape
    taps_ref = taps_out.ref
    count = devices // chans
    per = LANES // (taps_ref.shape[2] // chans)
    wide = per * LANES
    piece = LANES // per
    spread = chosen(wide, wide, lambda r: (r % LANES) // piece * LANES + r // LANES * piece + r % piece)
    fetch.wait()
    for frame in range(count):
        for side in range(chans // per):
            parts = []
            for k in range(per):
                parts.append(came_ref[frame * chans + side * per + k].reshape(groups * rows, LANES))
            result = dot_nt(jnp.concatenate(parts, axis=1), spread).astype(BF16)
            for slab in range(per):
                for group in range(groups):
                    if slab * groups + group < 9:
                        taps_ref[slab * groups + group, frame * rows : (frame + 1) * rows, side * LANES : (side + 1) * LANES] = result[
                            group * rows : (group + 1) * rows, slab * LANES : (slab + 1) * LANES
                        ]
    taps_out.send(0, 9, 0)
    taps_out.finish(0, 9, 9)


def turn_taps(taps, turned_ref):
    wide = taps.ref.shape[-1]
    taps.need_all()
    for kt in range(3):
        for kf in range(3):
            turned_ref[2 - kt, :, kf * wide : (kf + 1) * wide] = taps.ref[kt, kf * wide : (kf + 1) * wide]


def pack_wide(order, chans, me_ref, slabs, out_ref):
    devices, groups, rows, _ = out_ref.shape
    count = devices // chans
    per = LANES // (slabs[0].shape[1] // chans)
    wide = per * LANES
    piece = LANES // per
    gather = chosen(wide, wide, lambda r: (r % LANES) // piece * LANES + r // LANES * piece + r % piece)
    for group in range(groups):
        for side in range(chans // per):
            parts = []
            for slab in range(per):
                tap = slab * groups + group
                tap = tap if tap < 9 else 8
                parts.append(slabs[tap][:, side * LANES : (side + 1) * LANES])
            result = dot_nt(jnp.concatenate(parts, axis=1), gather).astype(BF16)
            for k in range(per):
                for frame in range(count):
                    at = code_of(order, {"chan": side * per + k, "frames": frame}) ^ me_ref[0]
                    out_ref[at, group] = result[frame * rows : (frame + 1) * rows, k * LANES : (k + 1) * LANES]


def unpack_first(chans, shard, count_zero, came, taps_ref, short_ref, vec_ref, pairs_ref, raw_ref):
    came_ref = came.ref
    came.need_all()
    devices = came_ref.shape[0]
    count = devices // chans
    ins, outs = short_ref.shape
    per = LANES // (outs // chans)
    rows = packed_rows(shard, per)
    wide = per * LANES
    piece = LANES // per
    spread = chosen(wide, wide, lambda r: (r % LANES) // piece * LANES + r // LANES * piece + r % piece)
    for frame in range(count):
        for side in range(chans // per):
            parts = [came_ref[(side * per + k) * count + frame, 0:rows] for k in range(per)]
            result = dot_nt(jnp.concatenate(parts, axis=1), spread)
            for slab in range(per):
                start = slab * rows
                size = min(rows, shard - start)
                if size > 0:
                    raw_ref[side, frame * shard + start : frame * shard + start + size] = result[
                        :size, slab * LANES : (slab + 1) * LANES
                    ]
    for tap in range(9):
        kt, kf = tap // 3, tap % 3
        for side in range(outs // LANES):
            lanes = slice(side * LANES, (side + 1) * LANES)
            taps_ref[kt, kf * ins : (kf + 1) * ins, lanes] = raw_ref[side, pl.ds(tap, ins, stride=9)].astype(BF16)
    for side in range(outs // LANES):
        short_ref[:, side * LANES : (side + 1) * LANES] = raw_ref[side, 9 * ins : 10 * ins].astype(BF16)
    parts = [jnp.sum(came_ref[:, rows + 16 * k : rows + 16 * (k + 1)].astype(F32), axis=0) for k in range(2)]
    sums = parts[0] + parts[1]
    average = sums[0:1] / count_zero
    vec_ref[0:1] = average
    vec_ref[1:2] = lax.rsqrt(sums[1:2] / count_zero - average * average + norm_epsilon)
    vec_ref[2:3] = sums[2:3]
    vec_ref[3:4] = sums[9:10]
    c = lax.broadcasted_iota(jnp.int32, (LANES, 2 * LANES), 1)
    r = lax.broadcasted_iota(jnp.int32, (LANES, 2 * LANES), 0)
    for side in range(2):
        place = (c == 2 * r + side).astype(BF16)
        spread_rows = [dot(part.astype(BF16), place) for part in (parts[0], parts[1])]
        both = spread_rows[0] + spread_rows[1]
        for k in range(3):
            for kind in range(2):
                row = both[2 + 7 * kind + 1 + 2 * k + side : 2 + 7 * kind + 2 + 2 * k + side]
                pairs_ref[k, kind : kind + 1] = row if side == 0 else pairs_ref[k, kind : kind + 1] + row


def turn_first(taps, short, turned_ref):
    ins, outs = short.ref.shape
    taps.need_all()
    short.need_all()
    for kt in range(3):
        turned_ref[2 - kt, 0:ins, 0:outs] = taps.ref[kt, ins : 2 * ins]
        turned_ref[2 - kt, 0:ins, outs:] = jnp.zeros((ins, outs), BF16)
        turned_ref[2 - kt, ins:, 0:outs] = taps.ref[kt, 2 * ins :]
        turned_ref[2 - kt, ins:, outs:] = taps.ref[kt, 0:ins]


def pack_first(order, chans, shard, me_ref, raw_ref, out_ref):
    devices, rows, _ = out_ref.shape
    count = devices // chans
    outs = raw_ref.shape[0] * LANES
    per = LANES // (outs // chans)
    wide = per * LANES
    piece = LANES // per
    gather = chosen(wide, wide, lambda r: (r % LANES) // piece * LANES + r // LANES * piece + r % piece)
    for frame in range(count):
        for side in range(chans // per):
            parts = [raw_ref[side, frame * shard + slab * rows : frame * shard + (slab + 1) * rows] for slab in range(per)]
            result = dot_nt(jnp.concatenate(parts, axis=1).astype(BF16), gather).astype(BF16)
            for k in range(per):
                at = code_of(order, {"chan": side * per + k, "frames": frame}) ^ me_ref[0]
                out_ref[at] = result[:, k * LANES : (k + 1) * LANES]


def packed_rows(shard, per):
    return -(-shard // (per * 16)) * 16


def frames_in(chan_ref, mains, edge_refs, total, target, body):
    parts = len(mains)
    for main in mains:
        main.need_all()
    for low, at, part in ((0, 0, 0), (total - HALO, HALO, parts - 1)):

        @pl.when(chan_ref[0] == part)
        def _():
            for main, edge_ref in zip(mains, edge_refs):
                main.ref[low : low + HALO] = edge_ref[at : at + HALO]

    def piece(at, chunk, _):
        cubes = jnp.concatenate([main.ref[pl.ds(at, chunk)] for main in mains], axis=1)
        body(cubes.reshape(chunk * cubes.shape[1], LANES), at, chunk)

    loop(0, total, target, piece, 2)


def lane_row(chan_ref, q, size):
    return (q // size ^ chan_ref[0]) * size + q % size


def frames_out(rows, count, out_ref, at):
    parts, _, size, _ = out_ref.shape
    cube = rows.reshape(count, parts * size, LANES)
    for s in range(parts):
        out_ref[s, pl.ds(at, count)] = cube[:, s * size : (s + 1) * size].astype(out_ref.dtype)


def pieces_of(total):
    return fit(total, 4)


def channels_of(ref, base, chunk, parity):
    return ref[pl.ds(base, chunk), parity].reshape(chunk * B1, ref.shape[-1])


def signal_kernel(parts, chan_ref, *rest):
    mains, edge_refs, x_out = rest[:parts], rest[parts : 2 * parts], rest[2 * parts]
    x_ref = x_out.ref
    size = mains[0].ref.shape[1]
    total = x_ref.shape[0]
    channels = x_ref.shape[-1]
    half = LANES // 2
    split = chosen(LANES, LANES, lambda r: r // half * half + r % B1 * 2 + r % half // B1)
    order = chosen(channels, channels, lambda r: r // half + lane_row(chan_ref, r % half, size) * 2)

    def turn(values, base, chunk):
        turned = dot_nt(split, values)
        for parity in range(2):
            pairs = []
            for pair in range(chunk // 2):
                lanes = turned[:, pair * LANES : (pair + 1) * LANES]
                even = lanes[parity * B1 : (parity + 1) * B1]
                odd = lanes[half + parity * B1 : half + (parity + 1) * B1]
                pairs.extend(halves_of(even, odd))
            x = dot(jnp.concatenate(pairs, axis=0).astype(BF16), order)
            x_ref[pl.ds(base, chunk), parity] = x.reshape(chunk, B1, channels).astype(BF16)

    frames_in(chan_ref, mains, edge_refs, total, 48, turn)
    x_out.send(0, total, 0)
    x_out.finish(0, total, total)


def first_kernel(own, prev_ref, next_ref, x, taps, short, vec_ref, h_out, s_out, copies_ref, cols_ref, acc_ref):
    total = x.ref.shape[0]
    channels = x.ref.shape[-1]
    norm = norm_rows(vec_ref)

    def build(base, chunk):
        acts = [activated(channels_of(x.ref, base, chunk, parity), norm) for parity in range(2)]
        below, _ = shifts(acts[1])
        put(cols_ref, base, chunk, jnp.concatenate([below, acts[0], acts[1]], axis=1))

    by_pieces([x], total, 12, build)
    acc_ref[...] = jnp.zeros_like(acc_ref)
    taps.need_all()
    short.need_all()

    def conv(base, chunk, number):
        result = taps_sum(cols_ref, taps.ref, (prev_ref, next_ref), base, chunk)
        put(h_out.ref, base, chunk, result)
        h_out.send(base, chunk, number)
        mine = own_rows(result, base, chunk, HALO, HALO + own)
        add_sums(acc_ref, mine, mine * mine)
        even = rows_of(cols_ref, base, chunk)[:, channels : 2 * channels]
        put(s_out.ref, base, chunk, dot(even, short.ref[...]))
        s_out.send(base, chunk, number)

    chunk = loop(1, total - 1, 47, conv)
    spread_sums(acc_ref, copies_ref)
    h_out.finish(1, total - 1, chunk)
    s_out.finish(1, total - 1, chunk)


def by_pieces(fetched, total, target, body):
    pieces = fetched[0].pieces
    size = total // pieces

    def piece(number, carry):
        for operand in fetched:
            operand.need(number)
        spans(number * size, size, target, lambda base, chunk, _: body(base, chunk))
        return carry

    lax.fori_loop(0, pieces, piece, 0)


def activate_into(h, norm, cols_ref):
    def build(base, chunk):
        act = activated(rows_of(h.ref, base, chunk), norm)
        below, above = shifts(act)
        put(cols_ref, base, chunk, jnp.concatenate([below, act, above], axis=1))

    by_pieces([h], cols_ref.shape[0], 24, build)


def forward_kernel(own, count, lead, target, with_short, prev_ref, next_ref, h, taps, *rest):
    if with_short:
        s, came_ref, pair_ref, out, copies_ref, cols_ref, acc_ref = rest
    else:
        came_ref, pair_ref, out, copies_ref, cols_ref, acc_ref = rest
    total = cols_ref.shape[0]
    activate_into(h, norm_of(came_ref, pair_ref, count), cols_ref)
    acc_ref[...] = jnp.zeros_like(acc_ref)
    taps.need_all()

    def conv(base, chunk, number):
        result = taps_sum(cols_ref, taps.ref, (prev_ref, next_ref), base, chunk)
        if with_short:
            pl.when(number == 0)(s.need_all)
            result = result + rows_of(s.ref, base, chunk).astype(F32)
        put(out.ref, base, chunk, result)
        out.send(base, chunk, number)
        mine = own_rows(result, base, chunk, HALO, HALO + own)
        add_sums(acc_ref, mine, mine * mine)

    chunk = loop(lead, total - lead, target, conv)
    spread_sums(acc_ref, copies_ref)
    out.finish(lead, total - lead, chunk)


def shift_into(value, base, chunk, cols_ref):
    below, above = shifts(value)
    put(cols_ref, base, chunk, jnp.concatenate([above, value, below], axis=1))


def top_kernel(parts, chan_ref, *rest):
    mains, edge_refs, e_out = rest[:parts], rest[parts : 2 * parts], rest[2 * parts]
    size = mains[0].ref.shape[1]
    total, _, wide = e_out.shape
    quarter = LANES // 4
    half = LANES // 2
    order = chosen(wide, wide, lambda r: r // half + lane_row(chan_ref, r % half, size) * 4)
    eye = chosen(LANES, LANES, same)

    def turn(values, base, chunk):
        turned = dot_nt(eye, values)
        frames = []
        for pair in range(chunk // 2):
            lanes = turned[:, pair * LANES : (pair + 1) * LANES]
            sides = [
                halves_of(
                    lanes[2 * side * quarter : (2 * side + 1) * quarter],
                    lanes[(2 * side + 1) * quarter : (2 * side + 2) * quarter],
                )
                for side in range(2)
            ]
            frames.extend([jnp.concatenate([sides[0][k], sides[1][k]], axis=1) for k in range(2)])
        put(e_out.ref, base, chunk, dot(jnp.concatenate(frames, axis=0).astype(BF16), order))

    frames_in(chan_ref, mains, edge_refs, total, 48, turn)
    e_out.send(0, total, 0)
    e_out.finish(0, total, total)


def top_back_kernel(prev_ref, next_ref, e, taps, q_out, cols_ref, turned_ref):
    total = q_out.shape[0]

    def build(base, chunk):
        shift_into(rows_of(e.ref, base, chunk).astype(F32), base, chunk, cols_ref)

    by_pieces([e], total, 24, build)
    turn_taps(taps, turned_ref)

    def back(base, chunk, number):
        put(q_out.ref, base, chunk, taps_sum(cols_ref, turned_ref, (prev_ref, next_ref), base, chunk, dot_nt))
        q_out.send(base, chunk, number)

    chunk = loop(3, total - 3, 30, back)
    q_out.finish(3, total - 3, chunk)


def top_norm_kernel(own, count, q, h, came_ref, pair_ref, dz_out, copies_ref, acc_ref):
    total = dz_out.shape[0]
    norm = norm_of(came_ref, pair_ref, count)
    acc_ref[...] = jnp.zeros_like(acc_ref)

    def back(base, chunk):
        dz, xhat = back_act(rows_of(q.ref, base, chunk).astype(F32), rows_of(h.ref, base, chunk), norm)
        put(dz_out.ref, base, chunk, dz)
        mine = own_rows(dz, base, chunk, HALO, HALO + own)
        add_sums(acc_ref, mine, own_rows(dz * xhat, base, chunk, HALO, HALO + own))

    by_pieces([q, h], total, 24, back)
    dz_out.send(0, total, 0)
    spread_sums(acc_ref, copies_ref)
    dz_out.finish(0, total, total)


def last_kernel(own, count, prev_ref, next_ref, h, taps, x, came_ref, pair_ref, y_ref, cols_ref):
    wide = cols_ref.shape[-1] // 3
    half = LANES // 2
    order = chosen(wide, wide, lambda r: r // half + r % half * 4)
    eye = chosen(LANES, LANES, same)
    activate_into(h, norm_of(came_ref, pair_ref, count), cols_ref)
    taps.need_all()
    x.need_all()

    def conv(base, chunk, _):
        result = taps_sum(cols_ref, taps.ref, (prev_ref, next_ref), base, chunk) + rows_of(x.ref, base, chunk).astype(F32)
        mixed = dot_nt(result.astype(BF16), order)
        cube = mixed.reshape(chunk, B1, wide)
        for pair in range(chunk // 2):
            stack = []
            for side in range(wide // LANES):
                lanes = slice(side * LANES, (side + 1) * LANES)
                stack.extend(halves_of(cube[2 * pair][:, lanes], cube[2 * pair + 1][:, lanes]))
            turned = dot_nt(eye, jnp.concatenate(stack, axis=0).astype(BF16))
            frames_out(turned, 2, y_ref, base - HALO + 2 * pair)

    loop(HALO, HALO + own, 28, conv, 2)


def middle_kernel(own, count, lead, target, with_top, prev_ref, next_ref, dz, h, *rest):
    if with_top:
        e, *rest = rest
    taps, low, back_ref, came_ref, pair_ref, low_came_ref, low_pair_ref, d_out, dz_out, copies_ref, cols_ref, acc_ref, turned_ref = rest
    total = cols_ref.shape[0]
    norm = norm_of(came_ref, pair_ref, count)
    low_norm = norm_of(low_came_ref, low_pair_ref, count)
    sums = came_sums(back_ref)

    def build(base, size):
        d = back_norm(rows_of(dz.ref, base, size), rows_of(h.ref, base, size), norm, sums, count)
        if with_top:
            d = d + rows_of(e.ref, base, size).astype(F32)
        put(d_out.ref, base, size, d)
        shift_into(d, base, size, cols_ref)

    by_pieces([dz, h, e] if with_top else [dz, h], total, 24, build)
    d_out.send(0, total, 0)
    acc_ref[...] = jnp.zeros_like(acc_ref)
    turn_taps(taps, turned_ref)

    def back(base, chunk, number):
        q = taps_sum(cols_ref, turned_ref, (prev_ref, next_ref), base, chunk, dot_nt)
        pl.when(number == 0)(low.need_all)
        new, xhat = back_act(q, rows_of(low.ref, base, chunk), low_norm)
        put(dz_out.ref, base, chunk, new)
        dz_out.send(base, chunk, number)
        mine = own_rows(new, base, chunk, HALO, HALO + own)
        add_sums(acc_ref, mine, mine * xhat)

    chunk = loop(lead, total - lead, target, back)
    spread_sums(acc_ref, copies_ref)
    d_out.finish(0, total, total)
    dz_out.finish(lead, total - lead, chunk)


def give(buffer_ref, keep_ref, send_ref, sems):
    half = keep_ref.shape[0]
    keep = pltpu.make_async_copy(buffer_ref.at[pl.ds(0, half)], keep_ref, sems.at[0])
    send = pltpu.make_async_copy(buffer_ref.at[pl.ds(half, half)], send_ref, sems.at[1])
    keep.start()
    send.start()
    keep.wait()
    send.wait()


def weight_kernel(
    own, count, order, chans, me_ref, prev_ref, next_ref, d, h, came_ref, pair_ref, keep_ref, send_ref,
    cols_ref, turned_ref, buffer_ref, sems,
):
    norm = norm_of(came_ref, pair_ref, count)
    wide = h.ref.shape[-1]

    def build(base, chunk):
        shift_into(rows_of(d.ref, base, chunk).astype(F32), base, chunk, cols_ref)

    by_pieces([d], cols_ref.shape[0], 24, build)
    h.need_all()

    def turn(base, chunk, _):
        u = activated(rows_of(h.ref, HALO + base, chunk), norm)
        columns = pl.ds(pl.multiple_of(base * B1, chunk * B1), chunk * B1)
        masked = (mask_frames(u, next_ref, HALO + base, chunk), u, mask_frames(u, prev_ref, HALO + base, chunk))
        for tap in range(3):
            turned_ref[tap, :, columns] = transposed(masked[tap].astype(BF16))

    loop(0, own, 28, turn, 4)
    slabs = []
    for tap in range(3):
        other = cols_ref[pl.ds(HALO + 1 - tap, own)].reshape(own * B1, cols_ref.shape[-1])
        grad = dot(turned_ref[tap], other).astype(BF16)
        slabs.extend([grad[:, k * wide : (k + 1) * wide] for k in range(3)])
    pack_wide(order, chans, me_ref, slabs, buffer_ref)
    give(buffer_ref, keep_ref, send_ref, sems)


def bottom_kernel(
    own, count, prev_ref, next_ref, dz, h, taps, short, e1, x, back_ref, came_ref, pair_ref, vec_ref,
    d_out, dz_out, copies_ref, cols_ref, acc_ref, turned_ref,
):
    total = cols_ref.shape[0]
    norm = norm_of(came_ref, pair_ref, count)
    low_norm = norm_rows(vec_ref)
    sums = came_sums(back_ref)
    channels = x.ref.shape[-1]

    def build(base, size):
        d = back_norm(rows_of(dz.ref, base, size), rows_of(h.ref, base, size), norm, sums, count)
        put(d_out.ref, base, size, d)
        _, above = shifts(d)
        put(cols_ref, base, size, jnp.concatenate([d, above], axis=1))

    by_pieces([dz, h], total, 24, build)
    d_out.send(0, total, 0)
    acc_ref[...] = jnp.zeros_like(acc_ref)
    turn_first(taps, short, turned_ref)
    e1.need_all()
    x.need_all()

    def back(base, chunk, number):
        q = taps_sum(cols_ref, turned_ref, (prev_ref, next_ref), base, chunk, dot_nt)
        r = dot_nt(rows_of(e1.ref, base, chunk), short.ref[...])
        parts = (q[:, :channels] + r, q[:, channels:])
        for parity in range(2):
            new, xhat = back_act(parts[parity], channels_of(x.ref, base, chunk, parity), low_norm)
            dz_out.ref[pl.ds(base - HALO, chunk), parity] = new.reshape(chunk, B1, channels).astype(BF16)
            add_sums(acc_ref, new, new * xhat)
        dz_out.send(base - HALO, chunk, number)

    chunk = loop(HALO, HALO + own, 28, back)
    spread_sums(acc_ref, copies_ref)
    d_out.finish(0, total, total)
    dz_out.finish(0, own, chunk)


def first_weight_kernel(
    own, order, chans, shard, me_ref, prev_ref, next_ref, d, x, e1, vec_ref, keep_ref, send_ref,
    cols_ref, turned_ref, raw_ref, buffer_ref, sems,
):
    norm = norm_rows(vec_ref)
    channels = x.ref.shape[-1]
    wide = d.ref.shape[-1]

    def build(base, size):
        value = rows_of(d.ref, base, size)
        _, above = shifts(value.astype(F32))
        put(cols_ref, base, size, jnp.concatenate([value, above.astype(BF16)], axis=1))

    by_pieces([d], cols_ref.shape[0], 24, build)
    x.need_all()
    e1.need_all()

    def turn(base, chunk, _):
        columns = pl.ds(pl.multiple_of(base * B1, chunk * B1), chunk * B1)
        for parity in range(2):
            u = activated(channels_of(x.ref, HALO + base, chunk, parity), norm)
            masked = (mask_frames(u, next_ref, HALO + base, chunk), u, mask_frames(u, prev_ref, HALO + base, chunk))
            for tap in range(3):
                turned_ref[tap, parity * channels : (parity + 1) * channels, columns] = transposed(masked[tap].astype(BF16))

    loop(0, own, 28, turn, 4)
    for tap in range(3):
        other = cols_ref[pl.ds(HALO + 1 - tap, own)].reshape(own * B1, cols_ref.shape[-1])
        grad = dot(turned_ref[tap], other)
        slabs = (grad[channels:, wide:], grad[:channels, :wide], grad[channels:, :wide])
        for kf in range(3):
            for side in range(wide // LANES):
                raw_ref[side, pl.ds(3 * tap + kf, channels, stride=9)] = slabs[kf][:, side * LANES : (side + 1) * LANES]
    short = dot(turned_ref[1, 0:channels], e1.ref[pl.ds(HALO, own)].reshape(own * B1, wide))
    rest = raw_ref.shape[1] - 10 * channels
    for side in range(wide // LANES):
        raw_ref[side, 9 * channels : 10 * channels] = short[:, side * LANES : (side + 1) * LANES]
        raw_ref[side, 10 * channels :] = jnp.zeros((rest, LANES), F32)
    pack_first(order, chans, shard, me_ref, raw_ref, buffer_ref)
    give(buffer_ref, keep_ref, send_ref, sems)


def input_kernel(own, count, dz, x, back_ref, vec_ref, out_ref):
    norm = norm_rows(vec_ref)
    sums = came_sums(back_ref)
    channels = x.ref.shape[-1]
    half = LANES // 2
    order = chosen(channels, channels, lambda r: r // half + r % half * 2)
    eye = chosen(LANES, LANES, same)
    split = chosen(LANES, LANES, lambda r: r // half * half + r % 2 * B1 + r % half // 2)
    dz.need_all()
    x.need_all()

    def build(base, chunk, _):
        mixed = []
        for parity in range(2):
            g = back_norm(
                channels_of(dz.ref, base, chunk, parity), channels_of(x.ref, HALO + base, chunk, parity), norm, sums, count
            )
            mixed.append(dot_nt(g.astype(BF16), order).reshape(chunk, B1, channels))
        for pair in range(chunk // 2):
            even, odd = [], []
            for parity in range(2):
                first, second = halves_of(mixed[parity][2 * pair], mixed[parity][2 * pair + 1])
                even.append(first)
                odd.append(second)
            stack = jnp.concatenate(even + odd, axis=0).astype(BF16)
            turned = dot_nt(eye, dot(split, stack).astype(BF16))
            frames_out(turned, 2, out_ref, base + 2 * pair)

    loop(0, own, 28, build, 2)


SMEM = pl.BlockSpec(memory_space=pltpu.SMEM)
VMEM = pl.BlockSpec(memory_space=pltpu.VMEM)
HBM = pl.BlockSpec(memory_space=pl.ANY)
DMA = pltpu.SemaphoreType.DMA


def run(kernel, scalars, fetched, operands, sent, outs, scratch, micros, plain=(), loose=()):
    arrays = [array for array, _ in fetched]
    buffers = [pltpu.VMEM(array.shape, array.dtype) for array in arrays] + [pltpu.VMEM(shape, kind) for shape, kind, _ in sent]
    sems = [DMA((pieces,)) for _, pieces in fetched] + [DMA((pieces,)) for _, _, pieces in sent]
    counts = (len(scalars), len(fetched), len(loose), len(operands), len(sent), len(plain), len(outs), len(scratch), len(buffers), len(sems))

    def whole(*refs):
        groups, at = [], 0
        for count in counts:
            groups.append(refs[at : at + count])
            at += count
        small, sources, left, inputs, targets, copied, results, own, held, marks = groups
        incoming = [Fetched(*triple) for triple in zip(sources, held, marks)]
        leaving = [Sent(*triple) for triple in zip(targets, held[len(incoming) :], marks[len(incoming) :])]
        for operand in incoming:
            operand.start()
        kernel(*small, *incoming, *left, *inputs, *leaving, *copied, *results, *own)

    made = [(shape, kind) for shape, kind, _ in sent] + list(plain) + list(outs)
    moved = sum(x.size * x.dtype.itemsize for x in arrays + list(operands))
    return pl.pallas_call(
        whole,
        in_specs=[SMEM] * len(scalars) + [HBM] * (len(arrays) + len(loose)) + [VMEM] * len(operands),
        out_specs=[HBM] * (len(sent) + len(plain)) + [VMEM] * len(outs),
        out_shape=[jax.ShapeDtypeStruct(shape, kind) for shape, kind in made],
        scratch_shapes=[pltpu.VMEM(*one) if isinstance(one, tuple) else one for one in scratch] + buffers + sems,
        compiler_params=pltpu.CompilerParams(vmem_limit_bytes=VMEM_BYTES),
        cost_estimate=pl.CostEstimate(flops=int(micros * 1.15e9), bytes_accessed=moved, transcendentals=0),
    )(*scalars, *arrays, *loose, *operands)


def norm_pair(params, norm_index):
    if norm_index == 0:
        return jnp.stack([params[0, 0], params[1, 0]])
    row_pair = params[:, 2 * norm_index - 1 : 2 * norm_index + 1]
    return jnp.transpose(row_pair, (0, 2, 1)).reshape(2, -1)


def pack_norms(vectors):
    blocks = [vectors[0][None]]
    for vector in vectors[1:]:
        blocks.append(vector.reshape(-1, 2).T)
    return jnp.concatenate(blocks, axis=0)


def adam_step(weight, moment, square, gradient, step_rate, decay_rate):
    moment_next = beta_first * moment + (1.0 - beta_first) * gradient
    square_next = beta_second * square + (1.0 - beta_second) * gradient * gradient
    corrected = moment_next / (1.0 - beta_first**STEP)
    divisor = jnp.sqrt(square_next / (1.0 - beta_second**STEP)) + adam_epsilon
    weight_next = weight - step_rate * (corrected / divisor + decay_rate * weight)
    return (weight_next, moment_next, square_next)


def body(
    signal,
    clip_ids,
    output_grad,
    first_weight,
    first_mean,
    first_square,
    wide_weight,
    wide_mean,
    wide_square,
    norm_params,
    norm_mean,
    norm_square,
):
    chans = lax.axis_size("chan")
    groups_of_frames = lax.axis_size("frames")
    devices = chans * groups_of_frames
    chan = lax.axis_index("chan")
    me = {"chan": chan, "frames": lax.axis_index("frames")}
    group = signal.shape[0]
    own = group // chans
    total = own + 2 * HALO
    frames = group * groups_of_frames
    in_local = signal.shape[1] // B0
    ins = in_local * chans
    wide_local = output_grad.shape[1] // B1
    wide = wide_local * chans
    columns = first_weight.shape[1]
    per = LANES // columns
    count_zero = frames * B0
    count = frames * B1

    order_grads = halves("chan", chans)[:-1] + halves("frames", groups_of_frames) + [("chan", 1)]
    signal_rows = signal.reshape(group, -1, LANES)
    signal_main, signal_edges, windows = to_frames(signal_rows)

    count_of_groups = lax.axis_size("frames")
    forward = [(i, i + 1) for i in range(count_of_groups - 1)]
    low = lax.ppermute(clip_ids[group - HALO - 1 :] + 1, "frames", forward)
    high = lax.ppermute(clip_ids[: HALO + 1] + 1, "frames", [(b, a) for a, b in forward])
    ids = lax.dynamic_slice_in_dim(jnp.concatenate([low, clip_ids + 1, high]), chan * own, total + 2, 0)
    masks = ((ids[:-2] == ids[1:-1]).astype(F32), (ids[2:] == ids[1:-1]).astype(F32))

    shard = first_weight.shape[0]
    packed = packed_rows(shard, per)
    first_send = jnp.pad(after(first_weight, *windows).astype(BF16), ((0, per * packed - shard), (0, 0)))
    first_send = jnp.transpose(first_send.reshape(per, packed, columns), (1, 0, 2)).reshape(packed, LANES)
    local = signal.astype(F32)
    local_sums = jnp.stack([jnp.sum(local, axis=0), jnp.sum(local * local, axis=0)]).reshape(2, in_local, B0).sum(axis=2)
    shared = jnp.where(me["frames"] == 0, norm_params.reshape(-1, in_local), 0.0)
    small = jnp.concatenate([local_sums, shared], axis=0)
    places = jnp.arange(LANES) // in_local == chan
    small = jnp.where(places[None], jnp.tile(small, (1, LANES // in_local)), 0.0)
    big = lax.reduce_precision(small, 8, 7)
    send = jnp.concatenate([first_send, big.astype(BF16), (small - big).astype(BF16)], axis=0)
    first_all = to_all(jnp.broadcast_to(send[None], (devices,) + send.shape))

    layers = wide_weight.shape[0]
    rows = wide_weight.shape[1] // 9
    slab_groups = -(-9 // per)
    wide_send = jnp.transpose(after(wide_weight, first_send).astype(BF16).reshape(layers, rows, 9, columns), (0, 2, 1, 3))
    wide_send = jnp.pad(wide_send, ((0, 0), (0, per * slab_groups - 9), (0, 0), (0, 0)))
    wide_send = jnp.transpose(wide_send.reshape(layers, per, slab_groups, rows, columns), (0, 2, 3, 1, 4))
    wide_send = wide_send.reshape(layers, slab_groups, rows, LANES)
    wide_all = lax.all_gather(wide_send, ("frames", "chan"), axis=0)

    chan_scalar = jnp.reshape(chan, (1,)).astype(jnp.int32)
    code_grads = jnp.reshape(code_of(order_grads, me), (1,)).astype(jnp.int32)

    cube = (total, B1, wide)
    cols = (total, B1, 3 * wide)
    lane_rows = signal_rows.shape[1]
    copies = ((devices, 1, 2 * wide), F32)
    acc = ((2, 8, wide), F32)

    pieces = pieces_of(total)

    def steps(low, target):
        return (total - 2 * low) // fit(total - 2 * low, target)

    def wide_taps(layer):
        taps = run(
            functools.partial(unpack_wide, layer, chans),
            (),
            [],
            (),
            [((9, wide, wide), BF16, 1)],
            [],
            [((devices, slab_groups, rows, LANES), BF16), DMA((1,))],
            3,
            loose=(wide_all,),
        )[0]
        return taps.reshape(3, 3 * wide, wide)

    taps_one, short_taps, vec_zero, pairs = run(
        functools.partial(unpack_first, chans, shard, count_zero),
        (),
        [(first_all, 1)],
        (),
        [],
        [((3, 3 * ins, wide), BF16), ((ins, wide), BF16), ((4, ins), F32), ((3, 2, wide), F32)],
        [((wide // LANES, 10 * ins, LANES), F32)],
        4,
    )
    (x_zero,) = run(
        functools.partial(signal_kernel, chans),
        (chan_scalar,),
        [(main, 1) for main in signal_main],
        signal_edges,
        [((total, 2, B1, ins), BF16, 1)],
        [],
        [],
        6,
    )
    top_main, top_edges, _ = to_frames(after(output_grad, x_zero).reshape(group, -1, LANES))
    hidden_one, shortcut, sums = run(
        functools.partial(first_kernel, own),
        masks,
        [(x_zero, pieces), (taps_one, 1), (short_taps, 1)],
        (vec_zero,),
        [(cube, BF16, steps(1, 47)), (cube, BF16, steps(1, 47))],
        [copies],
        [((total, B1, 3 * ins), BF16), acc],
        8,
    )
    came_one = to_all(sums)
    taps_two = wide_taps(0)
    residual, sums = run(
        functools.partial(forward_kernel, own, count, 2, 46, True),
        masks,
        [(hidden_one, pieces), (taps_two, 1), (shortcut, 1)],
        (came_one, pairs[0]),
        [(cube, BF16, steps(2, 46))],
        [copies],
        [(cols, BF16), acc],
        9,
    )
    came_two = to_all(sums)
    taps_three = wide_taps(1)
    (top,) = run(
        functools.partial(top_kernel, chans),
        (chan_scalar,),
        [(main, 1) for main in top_main],
        after(top_edges, residual),
        [(cube, BF16, 1)],
        [],
        [],
        10,
    )
    hidden_two, sums = run(
        functools.partial(forward_kernel, own, count, 3, 30, False),
        masks,
        [(residual, pieces), (after(taps_three, top), 1)],
        (came_two, pairs[1]),
        [(cube, BF16, steps(3, 30))],
        [copies],
        [(cols, BF16), acc],
        9,
    )
    came_three = to_all(sums)
    taps_four = wide_taps(2)
    (top_back,) = run(
        top_back_kernel,
        masks,
        [(after(top, hidden_two), pieces), (taps_four, 1)],
        (),
        [(cube, BF16, steps(3, 30))],
        [],
        [(cols, BF16), ((3, wide, 3 * wide), BF16)],
        7,
    )
    dz_three, sums = run(
        functools.partial(top_norm_kernel, own, count),
        (),
        [(top_back, pieces), (hidden_two, pieces)],
        (came_three, pairs[2]),
        [(cube, BF16, 1)],
        [copies],
        [acc],
        4,
    )
    back_three = to_all(sums)

    def weight_grad(came, pair, values, d):
        blocks = (devices, slab_groups, rows, LANES)
        kept = ((devices // 2,) + blocks[1:], BF16)
        return run(
            functools.partial(weight_kernel, own, count, order_grads, chans),
            (code_grads,) + masks,
            [(d, pieces), (values, 1)],
            (came, pair),
            [],
            [],
            [(cols, BF16), ((3, wide, own * B1), BF16), (blocks, BF16), DMA((2,))],
            9,
            [kept, kept],
        )

    four = weight_grad(came_three, pairs[2], hidden_two, after(top, dz_three))
    d_three, dz_two, sums = run(
        functools.partial(middle_kernel, own, count, 4, 44, False),
        masks,
        [(dz_three, pieces), (hidden_two, pieces), (after(taps_three, *four), 1), (residual, 1)],
        (back_three, came_three, pairs[2], came_two, pairs[1]),
        [(cube, BF16, 1), (cube, BF16, steps(4, 44))],
        [copies],
        [(cols, BF16), acc, ((3, wide, 3 * wide), BF16)],
        9,
    )
    back_two = to_all(sums)
    three = weight_grad(came_two, pairs[1], residual, d_three)
    (block_rows,) = run(
        functools.partial(last_kernel, own, count),
        masks,
        [(after(hidden_two, dz_two), pieces), (taps_four, 1), (residual, 1)],
        (came_three, pairs[2]),
        [],
        [((chans, own, lane_rows, LANES), BF16)],
        [(cols, BF16)],
        12,
    )
    low_top, dz_one, sums = run(
        functools.partial(middle_kernel, own, count, 5, 43, True),
        masks,
        [(dz_two, pieces), (residual, pieces), (top, pieces), (after(taps_two, block_rows, *three), 1), (hidden_one, 1)],
        (back_two, came_two, pairs[1], came_one, pairs[0]),
        [(cube, BF16, 1), (cube, BF16, steps(5, 43))],
        [copies],
        [(cols, BF16), acc, ((3, wide, 3 * wide), BF16)],
        9,
    )
    back_one = to_all(sums)
    two = weight_grad(came_one, pairs[0], hidden_one, low_top)
    d_one, dz_zero, sums = run(
        functools.partial(bottom_kernel, own, count),
        masks,
        [(dz_one, pieces), (hidden_one, pieces), (after(taps_one, *two), 1), (short_taps, 1), (low_top, 1), (x_zero, 1)],
        (back_one, came_one, pairs[0], vec_zero),
        [(cube, BF16, 1), ((own, 2, B1, ins), BF16, own // fit(own, 28))],
        [((devices, 1, 2 * ins), F32)],
        [((total, B1, 2 * wide), BF16), ((2, 8, ins), F32), ((3, 2 * ins, 2 * wide), BF16)],
        8,
    )
    back_zero = to_all(sums)
    one_blocks = (devices, packed, LANES)
    one_kept = ((devices // 2,) + one_blocks[1:], BF16)
    one = run(
        functools.partial(first_weight_kernel, own, order_grads, chans, shard),
        (code_grads,) + masks,
        [(d_one, pieces), (x_zero, 1), (low_top, 1)],
        (vec_zero,),
        [],
        [],
        [
            ((total, B1, 2 * wide), BF16),
            ((3, 2 * ins, own * B1), BF16),
            ((wide // LANES, 10 * ins + per * packed, LANES), F32),
            (one_blocks, BF16),
            DMA((2,)),
        ],
        8,
        [one_kept, one_kept],
    )
    (input_rows,) = run(
        functools.partial(input_kernel, own, count_zero),
        (),
        [(after(dz_zero, *one), 1), (x_zero, 1)],
        (back_zero, vec_zero),
        [],
        [((chans, own, lane_rows, LANES), BF16)],
        [],
        8,
    )

    block_out = lax.all_to_all(block_rows, "chan", 0, 0, tiled=True).reshape(group, -1).astype(F32)
    input_grad = lax.all_to_all(input_rows, "chan", 0, 0, tiled=True).reshape(group, -1).astype(F32)

    wide_sum = scatter_steps([two[0], three[0], four[0]], [two[1], three[1], four[1]], order_grads).astype(F32)
    wide_sum = jnp.transpose(wide_sum.reshape(3, slab_groups, rows, per, columns), (0, 3, 1, 2, 4))
    wide_sum = wide_sum.reshape(3, per * slab_groups, rows, columns)[:, :9]
    grad_wide = jnp.transpose(wide_sum, (0, 2, 1, 3)).reshape(wide_weight.shape)
    first_sum = scatter_steps([one[0]], [one[1]], order_grads).astype(F32)
    grad_first = jnp.transpose(first_sum.reshape(packed, per, columns), (1, 0, 2)).reshape(-1, columns)[:shard]

    norm_sums = [jnp.sum(came, axis=(0, 1)).reshape(2, -1) for came in (back_zero, back_one, back_two, back_three)]
    grad_norms = jnp.stack([pack_norms([s[1] for s in norm_sums]), pack_norms([s[0] for s in norm_sums])])
    grad_norms = lax.dynamic_slice_in_dim(grad_norms, chan * norm_params.shape[2], norm_params.shape[2], 2)
    own_squares = jnp.sum(grad_first * grad_first) + jnp.sum(grad_wide * grad_wide)
    own_squares = own_squares + jnp.where(lax.axis_index("frames") == 0, jnp.sum(grad_norms * grad_norms), 0.0)
    squares = jnp.sum(to_all(jnp.broadcast_to(own_squares, (devices, 1, LANES)))[:, 0, 0])
    grad_norm = jnp.sqrt(squares)
    factor = clip_limit / jnp.maximum(grad_norm, clip_limit)
    first_next, first_mean_next, first_square_next = adam_step(
        first_weight, first_mean, first_square, grad_first * factor, conv_rate, weight_decay
    )
    wide_next, wide_mean_next, wide_square_next = adam_step(
        wide_weight, wide_mean, wide_square, grad_wide * factor, conv_rate, weight_decay
    )
    norm_next, norm_mean_next, norm_square_next = adam_step(
        norm_params, norm_mean, norm_square, grad_norms * factor, norm_rate, 0.0
    )
    return (
        block_out,
        input_grad,
        grad_norm,
        first_next,
        first_mean_next,
        first_square_next,
        first_next.astype(BF16),
        wide_next,
        wide_mean_next,
        wide_square_next,
        wide_next.astype(BF16),
        norm_next,
        norm_mean_next,
        norm_square_next,
    )


def solution(mesh):
    rows = P("frames", "chan")
    deep = P(None, "frames", "chan")
    norms = P(None, None, "chan")
    in_specs = (rows, P("frames"), rows, rows, rows, rows, deep, deep, deep, norms, norms, norms)
    out_specs = (rows, rows, P(), rows, rows, rows, rows, deep, deep, deep, deep, norms, norms, norms)
    return jax.shard_map(body, mesh=mesh, in_specs=in_specs, out_specs=out_specs, check_vma=False)
```

time: 1660 us -> 401 us (0.24); the launches traced: 1640 us -> 398 us
  matrix products: 556 us -> 0 us
  local copies, waits for them, and re-layouts: 543 us -> 23.7 us
  blocking collectives: 275 us -> 0 us
  Pallas kernels: 0 us -> 157 us
  other arithmetic: 114 us -> 13.6 us
  starting transfers between devices: 42.2 us -> 123 us
  waiting for transfers between devices: 88.4 us -> 61.8 us
    dot_general x111 -> x0, matrix products: 556 us -> none  [the longest x36 250 us: conv_grad_input(): jnp.einsum('fbo,io->fbi', rows_used, taps[:, 3 * time_tap + freq_tap], pr...]
    slice x34 -> x10, local copies, waits for them, and re-layouts: 278 us -> 0.9 us  [the longest x3 0.47 us: body(): s[0]]
    psum x9 -> x0, blocking collectives: 199 us -> none  [the longest x4 86 us: statistics(): lax.psum((jnp.sum(values, axis=(0, 1)), jnp.sum(values * values, axis=(0,...]
    pallas_call x0 -> x20, Pallas kernels: none -> 157 us  [run(): pl.pallas_call(whole, in_specs=[SMEM] * len(scalars) + [HBM] * (len(array...]
    all_gather x2 -> x0, blocking collectives: 76.2 us -> none  [the longest x1 45.3 us: body(): lax.all_gather(wide_weight.astype(jnp.bfloat16), 'frames', axis=1, tiled=...]
    all_to_all x0 -> x11, starting transfers between devices: none -> 63.9 us  [the longest x9 56.8 us: to_all(): return lax.all_to_all(copies, BOTH, 0, 0, tiled=True)]
    another operation x17 -> x5, local copies, waits for them, and re-layouts: 59.1 us -> 1.03 us  [the longest x1 0.8 us: body(): wide_all = lax.all_gather(wide_send, ('frames', 'chan'), axis=0)]
    unnamed x381 -> x98, local copies, waits for them, and re-layouts: 61.5 us -> 14.9 us
  transfers between devices with their start and end apart: 28 -> 42, of which waited for: 6 -> 15; matrix products, arithmetic and copies ran while one was open for 45% -> 5% of each run, Pallas kernels for 0% -> 35%
where the time goes in v2:
time: 401 us; the launch traced here: 398 us
  Pallas kernels  157 us (39%)
  starting transfers between devices  123 us (31%)
  waiting for transfers between devices  61.8 us (15%)
  local copies, waits for them, and re-layouts  23.7 us (6%)
  between operations  19.3 us (5%)
  other arithmetic  13.6 us (3%)
    pallas_call x20, Pallas kernels, run(): pl.pallas_call(whole, in_specs=[SMEM] * len(scalars) + [HBM] * (len(array...  157 us
    all_to_all x9, starting transfers between devices, to_all(): return lax.all_to_all(copies, BOTH, 0, 0, tiled=True)  56.8 us
    ppermute x12, waiting for transfers between devices, scatter_steps(): came = [lax.ppermute(send, axis, swap) for send in sends]  30.8 us
    all_to_all x9, waiting for transfers between devices, to_all(): return lax.all_to_all(copies, BOTH, 0, 0, tiled=True)  18.7 us
    ppermute x1, starting transfers between devices, body(): low = lax.ppermute(clip_ids[group - HALO - 1:] + 1, 'frames', forward)  16.9 us
    ppermute x12, starting transfers between devices, scatter_steps(): came = [lax.ppermute(send, axis, swap) for send in sends]  15.5 us
    unnamed x98, local copies, waits for them, and re-layouts  14.9 us
    ppermute x2, starting transfers between devices, to_frames(): low = lax.ppermute(block[block.shape[0] - HALO:], 'frames', forward)  12.9 us
  transfers between devices with their start and end apart: 42, of which 15 were waited for; matrix products, arithmetic and copies ran while one was open for 5% of the time, Pallas kernels for 35%

profile of v2, /device:TPU:0, one launch (start us, length us, event | category | flops | bytes accessed | tf_op | source)
XLA Modules:
  0.0 397.7 jit_solution(11037428011757718504)
XLA Ops:
  17.1 6.1 %all-to-all-start = ((bf16[32,112,128]{2,1,0:T(8,128)(2,1)}), bf16[32,112,128]{2,1,0:T(8,128)(2,1)S(1)}, u32[]{:S(2)}, u32[]{:S(2)}) async-start(bf16[32,112,128]{2,1,0:T(8,128)(2,1)} %broadcast_in_dim.29), calls=%async_computation | async-start | bytes 1835008 | tf_op jit(solution)/shard_map/all_to_all | solution.py:34
  28.4 16.9 %collective-permute-start = (s32[7]{0:T(128)S(1)}, s32[7]{0:T(128)S(1)}, u32[]{:S(2)}, u32[]{:S(2)}) collective-permute-start(s32[7]{0:T(128)S(1)} %get-tuple-element.256), channel_id=1, source_target_pairs={{0,1},{1,2},{2,3},{3,4},{4,5},{5,6},{6,7},{8,9},{9,10},{10,11},{11... | collective-permute-start | bytes 92 | tf_op jit(solution)/shard_map/ppermute | solution.py:932
  62.9 9.2 %collective-permute-start.13 = (bf16[6,16,128]{2,1,0:T(8,128)(2,1)S(1)}, bf16[6,16,128]{2,1,0:T(8,128)(2,1)S(1)}, u32[]{:S(2)}, u32[]{:S(2)}) collective-permute-start(bf16[6,16,128]{2,1,0:T(8,128)(2,1)S(1)} %bitcast.108), channel_id=1, source_target_pairs={{0,1},{1,2},{2,3},{3,4},{4,5},{5,6},{6,7},{8,9},{9,10},{10,11},{11... | collective-permute-start | bytes 73736 | tf_op jit(solution)/shard_map/ppermute | solution.py:50
  85.9 8.3 %shard_map.229 = (bf16[96,32,256]{2,1,0:T(8,128)(2,1)}, bf16[96,32,256]{2,1,0:T(8,128)(2,1)}, f32[32,1,512]{2,1,0:T(1,128)}) custom-call(f32[96]{0:T(128)} %get-tuple-element.261.refs_0_.refs_1_, f32[96]{0:T(128)} %get-tuple-element.260.refs_1_.refs_2_, bf16[96,2,32,128]{3,2,1,0:T(8,128)(2,1)} %shard_map.227.refs_2_.refs_7_.refs_4_.refs_1_, ...), custom_call_target="tpu_custom_call" | custom-call | flops 9200000000 | bytes 2230272 | tf_op jit(solution)/shard_map/pallas_call | solution.py:860
  108.0 9.9 %shard_map.231 = (bf16[96,32,256]{2,1,0:T(8,128)(2,1)}, f32[32,1,512]{2,1,0:T(1,128)}) custom-call(f32[96]{0:T(128)} %get-tuple-element.261.refs_0_.refs_1_, f32[96]{0:T(128)} %get-tuple-element.260.refs_1_.refs_2_, bf16[96,32,256]{2,1,0:T(8,128)(2,1)} %get-tuple-element.63.refs_2_.refs_6_.refs_4_.refs_3_, bf16[3,768,256]{2,1,0:T(8,128)(2,1)} %bitcast.110, ...), custom_call_target="tpu_custom_call" | custom-call | flops 10350000128 | bytes 4392960 | tf_op jit(solution)/shard_map/pallas_call | solution.py:860
  117.9 16.8 %all-to-all-start.2 = ((f32[32,1,512]{2,1,0:T(1,128)}), f32[32,1,512]{2,1,0:T(1,128)S(1)}, u32[]{:S(2)}, u32[]{:S(2)}) async-start(f32[32,1,512]{2,1,0:T(1,128)} %get-tuple-element.75), calls=%async_computation.2 | async-start | bytes 131072 | tf_op jit(solution)/shard_map/all_to_all | solution.py:34
  147.7 9.3 %shard_map.234 = (bf16[96,32,256]{2,1,0:T(8,128)(2,1)}, f32[32,1,512]{2,1,0:T(1,128)}) custom-call(f32[96]{0:T(128)} %get-tuple-element.261.refs_0_.refs_1_, f32[96]{0:T(128)} %get-tuple-element.260.refs_1_.refs_2_, bf16[96,32,256]{2,1,0:T(8,128)(2,1)} %get-tuple-element.68.refs_2_.refs_5_.refs_4_.refs_3_, bf16[3,768,256]{2,1,0:T(8,128)(2,1)} %bitcast.112, ...), custom_call_target="tpu_custom_call" | custom-call | flops 10350000128 | bytes 2820096 | tf_op jit(solution)/shard_map/pallas_call | solution.py:860
  162.7 7.4 %shard_map.236.refs_0_ = bf16[96,32,256]{2,1,0:T(8,128)(2,1)} custom-call(f32[96]{0:T(128)} %get-tuple-element.261.refs_0_.refs_1_, f32[96]{0:T(128)} %get-tuple-element.260.refs_1_.refs_2_, bf16[96,32,256]{2,1,0:T(8,128)(2,1)} %shard_map.233.refs_2_.refs_3_.refs_4_, bf16[3,768,256]{2,1,0:T(8,128)(2,1)} %bitcast.114), custom_call_target="tpu_custom_call" | custom-call | flops 8049999872 | bytes 2752512 | tf_op jit(solution)/shard_map/pallas_call | solution.py:860
  170.7 6.2 %shard_map.237 = (bf16[96,32,256]{2,1,0:T(8,128)(2,1)}, f32[32,1,512]{2,1,0:T(1,128)}) custom-call(bf16[96,32,256]{2,1,0:T(8,128)(2,1)} %shard_map.236.refs_0_, bf16[96,32,256]{2,1,0:T(8,128)(2,1)} %get-tuple-element.86.refs_1_.refs_4_.refs_3_.refs_2_, f32[32,1,512]{2,1,0:T(1,128)} %copy-done.23, f32[2,256]{1,0:T(2,128)} %get-tuple-element.247.refs_3_.refs_6_.refs_8_), custom_call_target="tpu_custom_call" | custom-call | flops 4600000000 | bytes 3213312 | tf_op jit(solution)/shard_map/pallas_call | solution.py:860
  182.8 10.6 %shard_map.238 = (bf16[16,5,32,128]{3,2,1,0:T(8,128)(2,1)}, bf16[16,5,32,128]{3,2,1,0:T(8,128)(2,1)}) custom-call(s32[1]{0:T(128)} %bitcast.14.refs_0_, f32[96]{0:T(128)} %get-tuple-element.261.refs_0_.refs_1_, f32[96]{0:T(128)} %get-tuple-element.260.refs_1_.refs_2_, bf16[96,32,256]{2,1,0:T(8,128)(2,1)} %shard_map.233.refs_2_.refs_3_.refs_4_, ...), custom_call_target="tpu_custom_call" | custom-call | flops 10350000128 | bytes 3213312 | tf_op jit(solution)/shard_map/pallas_call | solution.py:860
  194.4 11.0 %shard_map.239 = (bf16[96,32,256]{2,1,0:T(8,128)(2,1)}, bf16[96,32,256]{2,1,0:T(8,128)(2,1)}, f32[32,1,512]{2,1,0:T(1,128)}) custom-call(f32[96]{0:T(128)} %get-tuple-element.261.refs_0_.refs_1_, f32[96]{0:T(128)} %get-tuple-element.260.refs_1_.refs_2_, bf16[96,32,256]{2,1,0:T(8,128)(2,1)} %get-tuple-element.79.refs_2_, ...), custom_call_target="tpu_custom_call" | custom-call | flops 10350000128 | bytes 6098944 | tf_op jit(solution)/shard_map/pallas_call | solution.py:860
  205.4 10.7 %shard_map.241 = (bf16[16,5,32,128]{3,2,1,0:T(8,128)(2,1)}, bf16[16,5,32,128]{3,2,1,0:T(8,128)(2,1)}) custom-call(s32[1]{0:T(128)} %bitcast.14.refs_0_, f32[96]{0:T(128)} %get-tuple-element.261.refs_0_.refs_1_, f32[96]{0:T(128)} %get-tuple-element.260.refs_1_.refs_2_, bf16[96,32,256]{2,1,0:T(8,128)(2,1)} %get-tuple-element.87.refs_3_, ...), custom_call_target="tpu_custom_call" | custom-call | flops 10350000128 | bytes 3213312 | tf_op jit(solution)/shard_map/pallas_call | solution.py:860
  216.4 11.4 %shard_map.240 = bf16[4,84,16,128]{3,2,1,0:T(8,128)(2,1)} custom-call(f32[96]{0:T(128)} %get-tuple-element.261.refs_0_.refs_1_, f32[96]{0:T(128)} %get-tuple-element.260.refs_1_.refs_2_, bf16[96,32,256]{2,1,0:T(8,128)(2,1)} %get-tuple-element.86.refs_1_.refs_4_.refs_3_.refs_2_, bf16[3,768,256]{2,1,0:T(8,128)(2,1)} %bitcast.115, ...), custom_call_target="tpu_custom_call" | custom-call | flops 13799999488 | bytes 4392960 | tf_op jit(solution)/shard_map/pallas_call | solution.py:860
  227.8 6.2 %all-to-all-start.6 = ((f32[32,1,512]{2,1,0:T(1,128)}), f32[32,1,512]{2,1,0:T(1,128)S(1)}, u32[]{:S(2)}, u32[]{:S(2)}) async-start(f32[32,1,512]{2,1,0:T(1,128)} %get-tuple-element.91), calls=%async_computation.6 | async-start | bytes 131072 | tf_op jit(solution)/shard_map/all_to_all | solution.py:34
  234.6 6.7 %all-to-all-done.6.refs_7_ = f32[32,1,512]{2,1,0:T(1,128)S(1)} async-done(((f32[32,1,512]{2,1,0:T(1,128)}), f32[32,1,512]{2,1,0:T(1,128)S(1)}, u32[]{:S(2)}, u32[]{:S(2)}) %all-to-all-start.6) | async-done | bytes 65568 | tf_op jit(solution)/shard_map/all_to_all | solution.py:34
  241.9 11.2 %shard_map.242 = (bf16[96,32,256]{2,1,0:T(8,128)(2,1)}, bf16[96,32,256]{2,1,0:T(8,128)(2,1)}, f32[32,1,512]{2,1,0:T(1,128)}) custom-call(f32[96]{0:T(128)} %get-tuple-element.261.refs_0_.refs_1_, f32[96]{0:T(128)} %get-tuple-element.260.refs_1_.refs_2_, bf16[96,32,256]{2,1,0:T(8,128)(2,1)} %get-tuple-element.85.refs_2_, ...), custom_call_target="tpu_custom_call" | custom-call | flops 10350000128 | bytes 7671808 | tf_op jit(solution)/shard_map/pallas_call | solution.py:860
  253.2 10.7 %shard_map.243 = (bf16[16,5,32,128]{3,2,1,0:T(8,128)(2,1)}, bf16[16,5,32,128]{3,2,1,0:T(8,128)(2,1)}) custom-call(s32[1]{0:T(128)} %bitcast.14.refs_0_, f32[96]{0:T(128)} %get-tuple-element.261.refs_0_.refs_1_, f32[96]{0:T(128)} %get-tuple-element.260.refs_1_.refs_2_, bf16[96,32,256]{2,1,0:T(8,128)(2,1)} %get-tuple-element.93.refs_3_.refs_6_.refs_5_, ...), custom_call_target="tpu_custom_call" | custom-call | flops 10350000128 | bytes 3213312 | tf_op jit(solution)/shard_map/pallas_call | solution.py:860
  267.1 6.8 %all-to-all-done.7.refs_8_ = f32[32,1,512]{2,1,0:T(1,128)S(1)} async-done(((f32[32,1,512]{2,1,0:T(1,128)}), f32[32,1,512]{2,1,0:T(1,128)S(1)}, u32[]{:S(2)}, u32[]{:S(2)}) %all-to-all-start.7) | async-done | bytes 65568 | tf_op jit(solution)/shard_map/all_to_all | solution.py:34
  274.5 9.5 %shard_map.244 = (bf16[96,32,256]{2,1,0:T(8,128)(2,1)}, bf16[84,2,32,128]{3,2,1,0:T(8,128)(2,1)}, f32[32,1,256]{2,1,0:T(1,128)}) custom-call(f32[96]{0:T(128)} %get-tuple-element.261.refs_0_.refs_1_, f32[96]{0:T(128)} %get-tuple-element.260.refs_1_.refs_2_, bf16[96,32,256]{2,1,0:T(8,128)(2,1)} %get-tuple-element.92.refs_2_, ...), custom_call_target="tpu_custom_call" | custom-call | flops 9200000000 | bytes 7081984 | tf_op jit(solution)/shard_map/pallas_call | solution.py:860
  286.9 9.6 %shard_map.245 = (bf16[16,80,128]{2,1,0:T(8,128)(2,1)}, bf16[16,80,128]{2,1,0:T(8,128)(2,1)}) custom-call(s32[1]{0:T(128)} %bitcast.14.refs_0_, f32[96]{0:T(128)} %get-tuple-element.261.refs_0_.refs_1_, f32[96]{0:T(128)} %get-tuple-element.260.refs_1_.refs_2_, bf16[96,32,256]{2,1,0:T(8,128)(2,1)} %get-tuple-element.99.refs_3_, ...), custom_call_target="tpu_custom_call" | custom-call | flops 9200000000 | bytes 4720640 | tf_op jit(solution)/shard_map/pallas_call | solution.py:860
  305.3 8.8 %shard_map.246 = bf16[4,84,16,128]{3,2,1,0:T(8,128)(2,1)} custom-call(bf16[84,2,32,128]{3,2,1,0:T(8,128)(2,1)} %get-tuple-element.102.refs_0_, bf16[96,2,32,128]{3,2,1,0:T(8,128)(2,1)} %shard_map.227.refs_2_.refs_7_.refs_4_.refs_1_, f32[32,1,256]{2,1,0:T(1,128)} %copy-done.18, f32[4,128]{1,0:T(4,128)} %get-tuple-element.62.refs_5_.refs_11_.refs_6_.refs_3_), custom_call_target="tpu_custom_call" | custom-call | flops 9200000000 | bytes 2983936 | tf_op jit(solution)/shard_map/pallas_call | solution.py:860
  316.6 8.1 %collective-permute-done.26 = bf16[8,15,32,128]{3,2,1,0:T(8,128)(2,1)} collective-permute-done((bf16[8,15,32,128]{3,2,1,0:T(8,128)(2,1)S(1)}, bf16[8,15,32,128]{3,2,1,0:T(8,128)(2,1)}, u32[]{:S(2)}, u32[]{:S(2)}) %collective-permute-start.26) | collective-permute-done | bytes 983072 | tf_op jit(solution)/shard_map/ppermute | solution.py:74
  329.3 10.6 %collective-permute-done.20 = bf16[4,80,128]{2,1,0:T(8,128)(2,1)S(1)} collective-permute-done((bf16[4,80,128]{2,1,0:T(8,128)(2,1)S(1)}, bf16[4,80,128]{2,1,0:T(8,128)(2,1)S(1)}, u32[]{:S(2)}, u32[]{:S(2)}) %collective-permute-start.20) | collective-permute-done | bytes 81952 | tf_op jit(solution)/shard_map/ppermute | solution.py:74
  359.5 6.1 %collective-permute-done.22 = bf16[1,80,128]{2,1,0:T(8,128)(2,1)S(1)} collective-permute-done((bf16[1,80,128]{2,1,0:T(8,128)(2,1)S(1)}, bf16[1,80,128]{2,1,0:T(8,128)(2,1)S(1)}, u32[]{:S(2)}, u32[]{:S(2)}) %collective-permute-start.22) | collective-permute-done | bytes 20512 | tf_op jit(solution)/shard_map/ppermute | solution.py:74
  (264 shorter events, 150.2 us)
Async XLA Ops:
  7.2 93.5 %all-gather.2.cloned.1.call-start = ((), (), s32[]{:S(2)}) async-start(), calls=%async_computation.11 | async-start | bytes 4055040 | tf_op jit(solution)/shard_map/all_gather | solution.py:958
  11.6 45.8 %collective-permute-start.2 = (bf16[96,16,128]{2,1,0:T(8,128)(2,1)S(1)}, bf16[96,16,128]{2,1,0:T(8,128)(2,1)}, u32[]{:S(2)}, u32[]{:S(2)}) collective-permute-start(bf16[96,16,128]{2,1,0:T(8,128)(2,1)S(1)} %get-tuple-element.228), channel_id=1, source_target_pairs={{0,8},{8,0},{16,24},{24,16},{1,9},{9,1},{17,25},{25,17},{2,10},{10... | collective-permute-start | bytes 1179656 | tf_op jit(solution)/shard_map/ppermute | solution.py:49
  12.2 45.3 %collective-permute-start.3 = (bf16[96,16,128]{2,1,0:T(8,128)(2,1)S(1)}, bf16[96,16,128]{2,1,0:T(8,128)(2,1)}, u32[]{:S(2)}, u32[]{:S(2)}) collective-permute-start(bf16[96,16,128]{2,1,0:T(8,128)(2,1)S(1)} %get-tuple-element.229), channel_id=1, source_target_pairs={{0,16},{8,24},{16,0},{24,8},{1,17},{9,25},{17,1},{25,9},{2,18},{10... | collective-permute-start | bytes 1179656 | tf_op jit(solution)/shard_map/ppermute | solution.py:49
  14.7 42.7 %collective-permute-start.4 = (bf16[96,16,128]{2,1,0:T(8,128)(2,1)S(1)}, bf16[96,16,128]{2,1,0:T(8,128)(2,1)}, u32[]{:S(2)}, u32[]{:S(2)}) collective-permute-start(bf16[96,16,128]{2,1,0:T(8,128)(2,1)S(1)} %get-tuple-element.227), channel_id=1, source_target_pairs={{0,24},{8,16},{16,8},{24,0},{1,25},{9,17},{17,9},{25,1},{2,26},{10... | collective-permute-start | bytes 1179656 | tf_op jit(solution)/shard_map/ppermute | solution.py:49
  17.1 65.1 %all-to-all-start = ((bf16[32,112,128]{2,1,0:T(8,128)(2,1)}), bf16[32,112,128]{2,1,0:T(8,128)(2,1)S(1)}, u32[]{:S(2)}, u32[]{:S(2)}) async-start(bf16[32,112,128]{2,1,0:T(8,128)(2,1)} %broadcast_in_dim.29), calls=%async_computation | async-start | bytes 1835008 | tf_op jit(solution)/shard_map/all_to_all | solution.py:34
  26.9 18.4 %collective-permute-start.6 = (bf16[6,16,128]{2,1,0:T(8,128)(2,1)S(1)}, bf16[6,16,128]{2,1,0:T(8,128)(2,1)S(1)}, u32[]{:S(2)}, u32[]{:S(2)}) collective-permute-start(bf16[6,16,128]{2,1,0:T(8,128)(2,1)S(1)} %bitcast.106), channel_id=1, source_target_pairs={{1,0},{2,1},{3,2},{4,3},{5,4},{6,5},{7,6},{9,8},{10,9},{11,10},{12... | collective-permute-start | bytes 73736 | tf_op jit(solution)/shard_map/ppermute | solution.py:51
  28.4 18.3 %collective-permute-start = (s32[7]{0:T(128)S(1)}, s32[7]{0:T(128)S(1)}, u32[]{:S(2)}, u32[]{:S(2)}) collective-permute-start(s32[7]{0:T(128)S(1)} %get-tuple-element.256), channel_id=1, source_target_pairs={{0,1},{1,2},{2,3},{3,4},{4,5},{5,6},{6,7},{8,9},{9,10},{10,11},{11... | collective-permute-start | bytes 92 | tf_op jit(solution)/shard_map/ppermute | solution.py:932
  74.9 63.1 %collective-permute-start.10 = (bf16[96,16,128]{2,1,0:T(8,128)(2,1)S(1)}, bf16[96,16,128]{2,1,0:T(8,128)(2,1)S(1)}, u32[]{:S(2)}, u32[]{:S(2)}) collective-permute-start(bf16[96,16,128]{2,1,0:T(8,128)(2,1)S(1)} %get-tuple-element.222), channel_id=1, source_target_pairs={{0,8},{8,0},{16,24},{24,16},{1,9},{9,1},{17,25},{25,17},{2,10},{10... | collective-permute-start | bytes 1179656 | tf_op jit(solution)/shard_map/ppermute | solution.py:49
  74.9 63.1 %collective-permute-start.11 = (bf16[96,16,128]{2,1,0:T(8,128)(2,1)S(1)}, bf16[96,16,128]{2,1,0:T(8,128)(2,1)S(1)}, u32[]{:S(2)}, u32[]{:S(2)}) collective-permute-start(bf16[96,16,128]{2,1,0:T(8,128)(2,1)S(1)} %get-tuple-element.223), channel_id=1, source_target_pairs={{0,16},{8,24},{16,0},{24,8},{1,17},{9,25},{17,1},{25,9},{2,18},{10... | collective-permute-start | bytes 1179656 | tf_op jit(solution)/shard_map/ppermute | solution.py:49
  76.9 61.2 %collective-permute-start.12 = (bf16[96,16,128]{2,1,0:T(8,128)(2,1)S(1)}, bf16[96,16,128]{2,1,0:T(8,128)(2,1)S(1)}, u32[]{:S(2)}, u32[]{:S(2)}) collective-permute-start(bf16[96,16,128]{2,1,0:T(8,128)(2,1)S(1)} %get-tuple-element.221), channel_id=1, source_target_pairs={{0,24},{8,16},{16,8},{24,0},{1,25},{9,17},{17,9},{25,1},{2,26},{10... | collective-permute-start | bytes 1179656 | tf_op jit(solution)/shard_map/ppermute | solution.py:49
  80.7 23.2 %collective-permute-start.15 = (bf16[12,16,128]{2,1,0:T(8,128)(2,1)S(1)}, bf16[12,16,128]{2,1,0:T(8,128)(2,1)S(1)}, u32[]{:S(2)}, u32[]{:S(2)}) collective-permute-start(bf16[12,16,128]{2,1,0:T(8,128)(2,1)S(1)} %constant_dynamic-update-slice_fusion.2.refs_5_), channel_id=1, source_target_pairs={{0,8},{8,0},{16,24},{24,16},{1,9},{9,1},{17,25},{25,17},{2,10},{10... | collective-permute-start | bytes 147464 | tf_op jit(solution)/shard_map/ppermute | solution.py:53
  81.0 36.8 %collective-permute-start.16 = (bf16[12,16,128]{2,1,0:T(8,128)(2,1)S(1)}, bf16[12,16,128]{2,1,0:T(8,128)(2,1)S(1)}, u32[]{:S(2)}, u32[]{:S(2)}) collective-permute-start(bf16[12,16,128]{2,1,0:T(8,128)(2,1)S(1)} %constant_dynamic-update-slice_fusion.2.refs_5_), channel_id=1, source_target_pairs={{0,16},{8,24},{16,0},{24,8},{1,17},{9,25},{17,1},{25,9},{2,18},{10... | collective-permute-start | bytes 147464 | tf_op jit(solution)/shard_map/ppermute | solution.py:53
  117.9 29.2 %all-to-all-start.2 = ((f32[32,1,512]{2,1,0:T(1,128)}), f32[32,1,512]{2,1,0:T(1,128)S(1)}, u32[]{:S(2)}, u32[]{:S(2)}) async-start(f32[32,1,512]{2,1,0:T(1,128)} %get-tuple-element.75), calls=%async_computation.2 | async-start | bytes 131072 | tf_op jit(solution)/shard_map/all_to_all | solution.py:34
  177.0 16.8 %all-to-all-start.4 = ((f32[32,1,512]{2,1,0:T(1,128)}), f32[32,1,512]{2,1,0:T(1,128)S(1)}, u32[]{:S(2)}, u32[]{:S(2)}) async-start(f32[32,1,512]{2,1,0:T(1,128)} %get-tuple-element.84), calls=%async_computation.4 | async-start | bytes 131072 | tf_op jit(solution)/shard_map/all_to_all | solution.py:34
  193.5 103.8 %collective-permute-start.25 = (bf16[16,5,32,128]{3,2,1,0:T(8,128)(2,1)}, bf16[16,5,32,128]{3,2,1,0:T(8,128)(2,1)S(1)}, u32[]{:S(2)}, u32[]{:S(2)}) collective-permute-start(bf16[16,5,32,128]{3,2,1,0:T(8,128)(2,1)} %get-tuple-element.82), channel_id=1, source_target_pairs={{0,8},{8,0},{16,24},{24,16},{1,9},{9,1},{17,25},{25,17},{2,10},{10... | collective-permute-start | bytes 1966088 | tf_op jit(solution)/shard_map/ppermute | solution.py:74
  216.1 81.4 %collective-permute-start.24 = (bf16[16,5,32,128]{3,2,1,0:T(8,128)(2,1)}, bf16[16,5,32,128]{3,2,1,0:T(8,128)(2,1)S(1)}, u32[]{:S(2)}, u32[]{:S(2)}) collective-permute-start(bf16[16,5,32,128]{3,2,1,0:T(8,128)(2,1)} %get-tuple-element.89), channel_id=1, source_target_pairs={{0,8},{8,0},{16,24},{24,16},{1,9},{9,1},{17,25},{25,17},{2,10},{10... | collective-permute-start | bytes 1966088 | tf_op jit(solution)/shard_map/ppermute | solution.py:74
  263.9 33.9 %collective-permute-start.23 = (bf16[16,5,32,128]{3,2,1,0:T(8,128)(2,1)}, bf16[16,5,32,128]{3,2,1,0:T(8,128)(2,1)}, u32[]{:S(2)}, u32[]{:S(2)}) collective-permute-start(bf16[16,5,32,128]{3,2,1,0:T(8,128)(2,1)} %get-tuple-element.95), channel_id=1, source_target_pairs={{0,8},{8,0},{16,24},{24,16},{1,9},{9,1},{17,25},{25,17},{2,10},{10... | collective-permute-start | bytes 1966088 | tf_op jit(solution)/shard_map/ppermute | solution.py:74
  284.1 17.6 %all-to-all-start.8 = ((f32[32,1,256]{2,1,0:T(1,128)}), f32[32,1,256]{2,1,0:T(1,128)S(1)}, u32[]{:S(2)}, u32[]{:S(2)}) async-start(f32[32,1,256]{2,1,0:T(1,128)} %get-tuple-element.103), calls=%async_computation.8 | async-start | bytes 65536 | tf_op jit(solution)/shard_map/all_to_all | solution.py:34
  297.0 17.8 %collective-permute-start.18 = (bf16[16,80,128]{2,1,0:T(8,128)(2,1)}, bf16[16,80,128]{2,1,0:T(8,128)(2,1)}, u32[]{:S(2)}, u32[]{:S(2)}) collective-permute-start(bf16[16,80,128]{2,1,0:T(8,128)(2,1)} %get-tuple-element.101), channel_id=1, source_target_pairs={{0,8},{8,0},{16,24},{24,16},{1,9},{9,1},{17,25},{25,17},{2,10},{10... | collective-permute-start | bytes 983048 | tf_op jit(solution)/shard_map/ppermute | solution.py:74
  299.9 24.8 %collective-permute-start.26 = (bf16[8,15,32,128]{3,2,1,0:T(8,128)(2,1)S(1)}, bf16[8,15,32,128]{3,2,1,0:T(8,128)(2,1)}, u32[]{:S(2)}, u32[]{:S(2)}) collective-permute-start(bf16[8,15,32,128]{3,2,1,0:T(8,128)(2,1)S(1)} %pad_maximum_fusion.1), channel_id=1, source_target_pairs={{0,1},{1,0},{2,3},{3,2},{4,5},{5,4},{6,7},{7,6},{8,9},{9,8},{10,11... | collective-permute-start | bytes 2949128 | tf_op jit(solution)/shard_map/ppermute | solution.py:74
  301.7 41.5 %all-to-all-start.5 = ((bf16[4,84,16,128]{3,2,1,0:T(8,128)(2,1)}), bf16[4,84,16,128]{3,2,1,0:T(8,128)(2,1)S(1)}, u32[]{:S(2)}, u32[]{:S(2)}) async-start(bf16[4,84,16,128]{3,2,1,0:T(8,128)(2,1)} %shard_map.240), calls=%async_computation.5 | async-start | bytes 2752512 | tf_op jit(solution)/shard_map/all_to_all | solution.py:1168
  326.1 16.6 %collective-permute-start.27 = (bf16[4,15,32,128]{3,2,1,0:T(8,128)(2,1)S(1)}, bf16[4,15,32,128]{3,2,1,0:T(8,128)(2,1)S(1)}, u32[]{:S(2)}, u32[]{:S(2)}) collective-permute-start(bf16[4,15,32,128]{3,2,1,0:T(8,128)(2,1)S(1)} %get-tuple-element.218), channel_id=1, source_target_pairs={{0,2},{1,3},{2,0},{3,1},{4,6},{5,7},{6,4},{7,5},{8,10},{9,11},{10,... | collective-permute-start | bytes 1474568 | tf_op jit(solution)/shard_map/ppermute | solution.py:74
  343.2 27.7 %all-to-all-start.9 = ((bf16[4,84,16,128]{3,2,1,0:T(8,128)(2,1)}), bf16[4,84,16,128]{3,2,1,0:T(8,128)(2,1)S(1)}, u32[]{:S(2)}, u32[]{:S(2)}) async-start(bf16[4,84,16,128]{3,2,1,0:T(8,128)(2,1)} %shard_map.246), calls=%async_computation.9 | async-start | bytes 2752512 | tf_op jit(solution)/shard_map/all_to_all | solution.py:1169
  348.4 17.2 %collective-permute-start.22 = (bf16[1,80,128]{2,1,0:T(8,128)(2,1)S(1)}, bf16[1,80,128]{2,1,0:T(8,128)(2,1)S(1)}, u32[]{:S(2)}, u32[]{:S(2)}) collective-permute-start(bf16[1,80,128]{2,1,0:T(8,128)(2,1)S(1)} %add_convert_fusion.20), channel_id=1, source_target_pairs={{0,16},{8,24},{16,0},{24,8},{1,17},{9,25},{17,1},{25,9},{2,18},{10... | collective-permute-start | bytes 61448 | tf_op jit(solution)/shard_map/ppermute | solution.py:74
  (59 other events, 414.5 us)
Sparse Core Ops, SparseCore 0:
  11.8 69.1 all-gather.1
